TPU v7x, 768 devices: a whole 4x8x12 slice. The times are simulated.
768 devices in a mesh: outer: 96 (over z_lo, y, core), inner: 8 (over z_hi, x).
Axes of the slice: x: 4, y: 8, z: 12 (z_hi: 2, z_lo: 6; z = z_hi * 6 + z_lo), core: 2. Of those that a mesh axis runs over, the one named last changes fastest.
Arguments:
- tokens: bfloat16 [196608, 8192], P(('outer', 'inner')), may hold values from -6 to 6
- cotangent: bfloat16 [196608, 48], P(('outer', 'inner')), may hold values from -0.0134887695 to 0.0134887695
- w_codes: bfloat16 [48, 64, 128], P(None, 'inner'), may hold values from -1 to 1
- w_scales: float32 [48, 64], P(None, 'inner'), may hold values from 0.01 to 0.04
Outputs:
- grad_shard: float32 [3072, 128], P(('outer', 'inner'))
All inputs are finite; a program needn't handle non-finite values.
Results may differ from a plain program's by a relative error of at most 0.018.
Values may be sent and summed in bfloat16 or wider, within the bound.
No kernel may reach another device: no remote copies, remote signals or barrier semaphores. Data moves between devices by JAX's collectives and lax.ppermute only.
A program may use at most 32 MiB of HBM per device.

v0:
```python
import jax
import jax.numpy as jnp
from jax import lax
from jax.sharding import PartitionSpec as P

BLOCK = 128


def slope(pre):
    sig = jax.nn.sigmoid(pre)
    return sig * (1.0 + pre * (1.0 - sig))


def on_device(tokens, cotangent, w_codes, w_scales):
    n_outer = lax.axis_size("outer")
    n_inner = lax.axis_size("inner")
    rows = w_codes.shape[0]
    width = tokens.shape[1]
    scales_wire = w_scales.astype(jnp.bfloat16)
    all_codes, all_scales = (
        lax.all_gather(w_codes, "inner", axis=1, tiled=True),
        lax.all_gather(scales_wire, "inner", axis=1, tiled=True),
    )
    weight = (all_codes.astype(jnp.float32) * all_scales.astype(jnp.float32)[..., None]).astype(
        jnp.bfloat16
    )
    weight = weight.reshape(rows, width)
    pre = lax.dot_general(
        tokens, weight, (((1,), (1,)), ((), ())), preferred_element_type=jnp.float32
    )
    delta = (cotangent.astype(jnp.float32) * slope(pre)).astype(jnp.bfloat16)
    local_grad = lax.dot_general(
        delta, tokens, (((0,), (0,)), ((), ())), preferred_element_type=jnp.float32
    )
    blocked = local_grad.reshape(n_outer, n_inner, -1, BLOCK)
    received = lax.all_to_all(
        blocked.astype(jnp.bfloat16), "inner", split_axis=1, concat_axis=1, tiled=True
    )
    partial_value = jnp.sum(received.astype(jnp.float32), axis=1)
    received_two = lax.all_to_all(
        partial_value.astype(jnp.bfloat16), "outer", split_axis=0, concat_axis=0, tiled=True
    )
    final = jnp.sum(received_two.astype(jnp.float32), axis=0)
    return final


def solution(mesh):
    in_specs = (
        P(("outer", "inner"), None),
        P(("outer", "inner"), None),
        P(None, "inner", None),
        P(None, "inner"),
    )
    out_specs = P(("outer", "inner"), None)
    return jax.shard_map(
        on_device, mesh=mesh, in_specs=in_specs, out_specs=out_specs, check_vma=False
    )
```

profile of v0, /device:TPU:1, one launch (start us, length us, event | category | flops | bytes accessed | tf_op | source)
XLA Modules:
  0.0 183.5 jit_solution(4682735404738262069)
XLA Ops:
  0.0 0.7 convert_element_type.31
  0.7 50.9 %all_gather.7 = bf16[48,64]{0,1:T(8,128)(2,1)S(1)} all-gather(bf16[48,8]{0,1:T(8,128)(2,1)S(1)} %convert_element_type.31), channel_id=1, replica_groups=mesh['outer'=96,'inner'=8] {'inner'}, dimensions={1}, use_global_device_ids=true | all-gather | bytes 6912 | tf_op jit(solution)/shard_map/all_gather | solution.py:22
  51.6 0.1 copy.16
  51.7 60.8 %all_gather.6 = bf16[48,64,128]{2,1,0:T(8,128)(2,1)S(1)} all-gather(bf16[48,8,128]{2,1,0:T(8,128)(2,1)} %param.6), channel_id=1, replica_groups=mesh['outer'=96,'inner'=8] {'inner'}, dimensions={1}, use_global_device_ids=true | all-gather | bytes 884736 | tf_op jit(solution)/shard_map/all_gather | solution.py:21
  112.5 0.5 multiply_convert_fusion
  112.9 6.5 %convolution_convert_fusion = bf16[48,8192]{1,0:T(8,128)(2,1)S(1)} fusion(bf16[256,8192]{1,0:T(8,128)(2,1)} %param.4, bf16[6,8,64,128]{3,2,1,0:T(8,128)(2,1)S(1)} %bitcast.16, bf16[256,48]{0,1:T(8,128)(2,1)} %param.5), kind=kOutput, calls=%fused_computation | convolution fusion | flops 403169280 | bytes 5791744 | tf_op jit(solution)/shard_map/dot_general | solution.py:32
  119.4 0.6 convert_element_type.36
  120.0 0.3 copy.17
  120.3 25.0 %all_to_all.10 = bf16[96,8,4,128]{3,2,0,1:T(4,128)(2,1)S(1)} all-to-all(bf16[96,8,4,128]{3,2,0,1:T(4,128)(2,1)S(1)} %copy.17), channel_id=1, replica_groups=mesh['outer'=96,'inner'=8] {'inner'}, dimensions={1} | all-to-all | bytes 1572864 | tf_op jit(solution)/shard_map/all_to_all | solution.py:36
  145.3 0.4 reduce_sum.21
  145.7 37.2 %all_to_all.11 = bf16[96,4,128]{2,1,0:T(4,128)(2,1)S(1)} all-to-all(bf16[96,4,128]{2,1,0:T(4,128)(2,1)S(1)} %reduce_sum.21), channel_id=1, replica_groups=mesh['outer'=96,'inner'=8] {'outer'}, dimensions={0} | all-to-all | bytes 196608 | tf_op jit(solution)/shard_map/all_to_all | solution.py:40
  182.9 0.6 convert_reduce_fusion
  (1 shorter events, 0.0 us)
where the time goes:
time: 184 us
  blocking collectives  174 us (95%)
  matrix products  6.45 us (4%)
  other arithmetic  2.17 us (1%)
    all_gather x1, blocking collectives, on_device(): lax.all_gather(w_codes, 'inner', axis=1, tiled=True)  60.8 us
    all_gather x1, blocking collectives, on_device(): lax.all_gather(scales_wire, 'inner', axis=1, tiled=True)  50.9 us
    all_to_all x1, blocking collectives, on_device(): lax.all_to_all(partial_value.astype(jnp.bfloat16), 'outer', split_axis=0,...  37.2 us
    all_to_all x1, blocking collectives, on_device(): lax.all_to_all(blocked.astype(jnp.bfloat16), 'inner', split_axis=1, conca...  25 us
    dot_general x1, matrix products, on_device(): lax.dot_general(delta, tokens, (((0,), (0,)), ((), ())), preferred_elemen...  6.45 us

commit v1 on v0

v1 whole, which is shorter than its diff:
```python
import jax
import jax.numpy as jnp
from jax import lax
from jax.sharding import Mesh, PartitionSpec as P

BLOCK = 128
Z_LO, Y, CORE, Z_HI, X = 6, 8, 2, 2, 4
ROWS = 48
HALF_ROWS = ROWS // CORE
SHARD = 1024
PIECE = 512


def slope(pre):
    sig = jax.nn.sigmoid(pre)
    return sig * (1.0 + pre * (1.0 - sig))


def gather_weight(w_codes, w_scales):
    core = lax.axis_index("core")
    z_hi = lax.axis_index("z_hi")
    codes = lax.dynamic_slice_in_dim(w_codes, core * HALF_ROWS, HALF_ROWS, 0)
    scales = lax.dynamic_slice_in_dim(w_scales, core * HALF_ROWS, HALF_ROWS, 0)
    mine = (codes.astype(jnp.float32) * scales[..., None]).astype(jnp.bfloat16)
    mine = mine.reshape(HALF_ROWS, SHARD)
    mirror = [
        (lo * Z_HI + hi, (Z_LO - 1 - lo) * Z_HI + (1 - hi))
        for lo in range(Z_LO)
        for hi in range(Z_HI)
    ]
    other = lax.ppermute(mine, ("z_lo", "z_hi"), mirror)
    first = jnp.where(z_hi == 0, mine, other)
    second = jnp.where(z_hi == 0, other, mine)
    both = jnp.stack([first, second])
    return lax.all_gather(both, "x", axis=0)


def on_device(tokens, cotangent, w_codes, w_scales):
    core = lax.axis_index("core")
    swap = [(0, 1), (1, 0)]
    my_rows = gather_weight(w_codes, w_scales)
    their_rows = lax.ppermute(my_rows, "core", swap)
    rows = jnp.where(
        core == 0, jnp.stack([my_rows, their_rows]), jnp.stack([their_rows, my_rows])
    )
    weight = rows.transpose(0, 3, 2, 1, 4).reshape(ROWS, -1)
    pre = lax.dot_general(
        tokens, weight, (((1,), (1,)), ((), ())), preferred_element_type=jnp.float32
    )
    delta = (cotangent.astype(jnp.float32) * slope(pre)).astype(jnp.bfloat16)
    local_grad = lax.dot_general(
        delta, tokens, (((0,), (0,)), ((), ())), preferred_element_type=jnp.float32
    ).astype(jnp.bfloat16)
    width = local_grad.shape[1] // CORE
    keep = lax.dynamic_slice_in_dim(local_grad, core * width, width, 1)
    give = lax.dynamic_slice_in_dim(local_grad, (1 - core) * width, width, 1)
    got = lax.ppermute(give, "core", swap)
    chip = (keep.astype(jnp.float32) + got.astype(jnp.float32)).astype(jnp.bfloat16)
    by_x = chip.reshape(ROWS, Z_HI, X, PIECE).transpose(2, 0, 1, 3).reshape(X, ROWS, Z_HI * PIECE)
    from_x = lax.all_to_all(by_x, "x", split_axis=0, concat_axis=0, tiled=True)
    row_sum = jnp.sum(from_x.astype(jnp.float32), axis=0).astype(jnp.bfloat16)
    by_yz = row_sum.reshape(ROWS * Z_HI, PIECE // BLOCK, BLOCK)
    from_yz = lax.all_to_all(by_yz, ("z_lo", "y", "z_hi"), split_axis=0, concat_axis=0, tiled=True)
    return jnp.sum(from_yz.astype(jnp.float32), axis=0)


def solution(mesh):
    fine = Mesh(
        mesh.devices.reshape(Z_LO, Y, CORE, Z_HI, X), ("z_lo", "y", "core", "z_hi", "x")
    )
    outer, inner = ("z_lo", "y", "core"), ("z_hi", "x")
    in_specs = (
        P(outer + inner, None),
        P(outer + inner, None),
        P(None, inner, None),
        P(None, inner),
    )
    return jax.shard_map(
        on_device, mesh=fine, in_specs=in_specs, out_specs=P(outer + inner, None), check_vma=False
    )
```

time: 184 us -> 89.5 us (0.49)
  blocking collectives: 174 us -> 47.9 us
  starting transfers between devices: 0 us -> 22 us
  waiting for transfers between devices: 0 us -> 6.93 us
  local copies, waits for them, and re-layouts: 0.92 us -> 2.98 us
    all_gather x2 -> x1, blocking collectives: 112 us -> 10.6 us  [gather_weight(): return lax.all_gather(both, 'x', axis=0)]
    all_to_all x2, blocking collectives: 62.3 us -> 37.3 us  [the longest x1 26.6 us: on_device(): lax.all_to_all(by_yz, ('z_lo', 'y', 'z_hi'), split_axis=0, concat_axis=0,...]
    ppermute x0 -> x3, starting transfers between devices: none -> 22 us  [the longest x1 15.1 us: gather_weight(): other = lax.ppermute(mine, ('z_lo', 'z_hi'), mirror)]
    ppermute x0 -> x3, waiting for transfers between devices: none -> 6.93 us  [the longest x1 4.28 us: gather_weight(): other = lax.ppermute(mine, ('z_lo', 'z_hi'), mirror)]
  transfers between devices with their start and end apart: 0 -> 3, of which waited for: 0 -> 3; matrix products, arithmetic and copies ran while one was open for 0% -> 0% of each run, Pallas kernels for 0% -> 0%
where the time goes in v1:
time: 89.5 us; the launch traced here: 88.2 us
  blocking collectives  47.9 us (54%)
  starting transfers between devices  22 us (25%)
  waiting for transfers between devices  6.93 us (8%)
  matrix products  6.41 us (7%)
  local copies, waits for them, and re-layouts  2.98 us (3%)
  other arithmetic  1.8 us (2%)
    all_to_all x1, blocking collectives, on_device(): lax.all_to_all(by_yz, ('z_lo', 'y', 'z_hi'), split_axis=0, concat_axis=0,...  26.6 us
    ppermute x1, starting transfers between devices, gather_weight(): other = lax.ppermute(mine, ('z_lo', 'z_hi'), mirror)  15.1 us
    all_to_all x1, blocking collectives, on_device(): from_x = lax.all_to_all(by_x, 'x', split_axis=0, concat_axis=0, tiled=True)  10.8 us
    all_gather x1, blocking collectives, gather_weight(): return lax.all_gather(both, 'x', axis=0)  10.6 us
    dot_general x1, matrix products, on_device(): lax.dot_general(delta, tokens, (((0,), (0,)), ((), ())), preferred_elemen...  6.41 us
    ppermute x1, starting transfers between devices, on_device(): their_rows = lax.ppermute(my_rows, 'core', swap)  4.62 us
    ppermute x1, waiting for transfers between devices, gather_weight(): other = lax.ppermute(mine, ('z_lo', 'z_hi'), mirror)  4.28 us
    ppermute x1, starting transfers between devices, on_device(): got = lax.ppermute(give, 'core', swap)  2.28 us
  transfers between devices with their start and end apart: 3, of which 3 were waited for; matrix products, arithmetic and copies ran while one was open for 0% of the time, Pallas kernels for 0%

profile of v1, /device:TPU:1, one launch (start us, length us, event | category | flops | bytes accessed | tf_op | source)
XLA Modules:
  0.0 88.2 jit_solution(5809870329649798243)
XLA Ops:
  0.0 0.0 copy-start
  0.0 0.0 copy-start.1
  0.0 0.7 copy-done
  0.7 0.1 constant_dynamic-slice_fusion.1
  0.8 0.1 copy.25
  0.8 0.9 %multiply_convert_fusion = bf16[24,8,128]{2,1,0:T(8,128)(2,1)S(1)} fusion(f32[24,8]{1,0:T(8,128)S(1)} %copy.25, bf16[48,8,128]{2,1,0:T(8,128)(2,1)} %param.6, s32[]{:T(128)S(6)} %select_n.32), kind=kLoop, calls=%fused_computation.8 | loop fusion | flops 73728 | bytes 99076 | tf_op jit(solution)/shard_map/convert_element_type | solution.py:24
  1.7 15.1 %collective-permute-start = (bf16[24,1024]{1,0:T(8,128)(2,1)S(1)}, bf16[24,1024]{1,0:T(8,128)(2,1)S(1)}, u32[]{:S(2)}, u32[]{:S(2)}) collective-permute-start(bf16[24,1024]{1,0:T(8,128)(2,1)S(1)} %bitcast.35), channel_id=1, source_target_pairs={{0,644},{4,640},{128,516},{132,512},{256,388},{260,384},{384,260},... | collective-permute-start | bytes 147464 | tf_op jit(solution)/shard_map/ppermute | solution.py:31
  16.9 4.3 %collective-permute-done = bf16[24,1024]{1,0:T(8,128)(2,1)S(1)} collective-permute-done((bf16[24,1024]{1,0:T(8,128)(2,1)S(1)}, bf16[24,1024]{1,0:T(8,128)(2,1)S(1)}, u32[]{:S(2)}, u32[]{:S(2)}) %collective-permute-start) | collective-permute-done | bytes 49184 | tf_op jit(solution)/shard_map/ppermute | solution.py:31
  21.2 10.6 %all-gather = bf16[8,24,1024]{2,1,0:T(8,128)(2,1)S(1)} all-gather(bf16[2,24,1024]{2,1,0:T(8,128)(2,1)S(1)} %pad_maximum_fusion), channel_id=2, replica_groups=mesh['z_lo'=6,'y'=8,'core'=2,'z_hi'=2,'x'=4] {'x'}, dimensions={0}, use_global_device_ids=true | all-gather | bytes 491520 | tf_op jit(solution)/shard_map/all_gather | solution.py:35
  31.8 4.6 %collective-permute-start.1 = (bf16[4,2,24,1024]{3,2,1,0:T(8,128)(2,1)S(1)}, bf16[4,2,24,1024]{3,2,1,0:T(8,128)(2,1)S(1)}, u32[]{:S(2)}, u32[]{:S(2)}) collective-permute-start(bf16[4,2,24,1024]{3,2,1,0:T(8,128)(2,1)S(1)} %bitcast.30), channel_id=1, source_target_pairs={{0,8},{8,0},{1,9},{9,1},{2,10},{10,2},{3,11},{11,3},{4,12},{12,4},... | collective-permute-start | bytes 1179656 | tf_op jit(solution)/shard_map/ppermute | solution.py:42
  36.5 1.3 %collective-permute-done.1 = bf16[4,2,24,1024]{3,2,1,0:T(8,128)(2,1)S(1)} collective-permute-done((bf16[4,2,24,1024]{3,2,1,0:T(8,128)(2,1)S(1)}, bf16[4,2,24,1024]{3,2,1,0:T(8,128)(2,1)S(1)}, u32[]{:S(2)}, u32[]{:S(2)}) %collective-permute-start.1) | collective-permute-done | bytes 393248 | tf_op jit(solution)/shard_map/ppermute | solution.py:42
  37.8 0.1 fusion
  37.9 0.6 copy.26
  38.5 0.6 reshape.17
  39.1 0.0 copy-done.1
  39.1 6.4 %convolution_convert_fusion = bf16[48,8192]{1,0:T(8,128)(2,1)S(1)} fusion(bf16[256,8192]{1,0:T(8,128)(2,1)} %param.4, bf16[48,8192]{1,0:T(8,128)(2,1)S(1)} %reshape.17, bf16[256,48]{0,1:T(8,128)(2,1)S(1)} %copy-done.1), kind=kOutput, calls=%fused_computation | convolution fusion | flops 403169280 | bytes 5791744 | tf_op jit(solution)/shard_map/dot_general | solution.py:51
  45.6 2.3 %collective-permute-start.2 = (bf16[48,4096]{1,0:T(8,128)(2,1)S(1)}, bf16[48,4096]{1,0:T(8,128)(2,1)S(1)}, u32[]{:S(2)}, u32[]{:S(2)}) collective-permute-start(bf16[48,4096]{1,0:T(8,128)(2,1)S(1)} %constant_dynamic-slice_fusion), channel_id=1, source_target_pairs={{0,8},{8,0},{1,9},{9,1},{2,10},{10,2},{3,11},{11,3},{4,12},{12,4},... | collective-permute-start | bytes 1179656 | tf_op jit(solution)/shard_map/ppermute | solution.py:57
  47.9 1.3 %collective-permute-done.2 = bf16[48,4096]{1,0:T(8,128)(2,1)S(1)} collective-permute-done((bf16[48,4096]{1,0:T(8,128)(2,1)S(1)}, bf16[48,4096]{1,0:T(8,128)(2,1)S(1)}, u32[]{:S(2)}, u32[]{:S(2)}) %collective-permute-start.2) | collective-permute-done | bytes 393248 | tf_op jit(solution)/shard_map/ppermute | solution.py:57
  49.2 0.1 add_convert_fusion
  49.3 0.3 reshape.18
  49.6 0.3 copy.37
  49.9 0.3 reshape.19
  50.2 10.8 %all_to_all.10 = bf16[4,48,1024]{2,1,0:T(8,128)(2,1)S(1)} all-to-all(bf16[4,48,1024]{2,1,0:T(8,128)(2,1)S(1)} %reshape.19), channel_id=1, replica_groups=mesh['z_lo'=6,'y'=8,'core'=2,'z_hi'=2,'x'=4] {'x'}, dimensions={0} | all-to-all | bytes 786432 | tf_op jit(solution)/shard_map/all_to_all | solution.py:60
  60.9 0.1 reduce_sum.21
  61.1 26.6 %all_to_all.11 = bf16[96,4,128]{2,1,0:T(4,128)(2,1)S(1)} all-to-all(bf16[96,4,128]{2,1,0:T(4,128)(2,1)S(1)} %reshape.20), channel_id=1, replica_groups=mesh['z_lo'=6,'y'=8,'core'=2,'z_hi'=2,'x'=4] {'z_lo','y','z_hi'}, dimensions={0} | all-to-all | bytes 196608 | tf_op jit(solution)/shard_map/all_to_all | solution.py:63
  87.6 0.6 convert_reduce_fusion
  (5 shorter events, 0.1 us)
Async XLA Ops:
  0.0 0.7 copy-start
  0.0 39.1 %copy-start.1 = (bf16[256,48]{0,1:T(8,128)(2,1)S(1)}, bf16[256,48]{0,1:T(8,128)(2,1)}, u32[]{:S(2)}) copy-start(bf16[256,48]{0,1:T(8,128)(2,1)} %param.5) | copy-start | bytes 73732
  1.7 19.4 %collective-permute-start = (bf16[24,1024]{1,0:T(8,128)(2,1)S(1)}, bf16[24,1024]{1,0:T(8,128)(2,1)S(1)}, u32[]{:S(2)}, u32[]{:S(2)}) collective-permute-start(bf16[24,1024]{1,0:T(8,128)(2,1)S(1)} %bitcast.35), channel_id=1, source_target_pairs={{0,644},{4,640},{128,516},{132,512},{256,388},{260,384},{384,260},... | collective-permute-start | bytes 147464 | tf_op jit(solution)/shard_map/ppermute | solution.py:31
  31.8 6.0 %collective-permute-start.1 = (bf16[4,2,24,1024]{3,2,1,0:T(8,128)(2,1)S(1)}, bf16[4,2,24,1024]{3,2,1,0:T(8,128)(2,1)S(1)}, u32[]{:S(2)}, u32[]{:S(2)}) collective-permute-start(bf16[4,2,24,1024]{3,2,1,0:T(8,128)(2,1)S(1)} %bitcast.30), channel_id=1, source_target_pairs={{0,8},{8,0},{1,9},{9,1},{2,10},{10,2},{3,11},{11,3},{4,12},{12,4},... | collective-permute-start | bytes 1179656 | tf_op jit(solution)/shard_map/ppermute | solution.py:42
  45.6 3.6 %collective-permute-start.2 = (bf16[48,4096]{1,0:T(8,128)(2,1)S(1)}, bf16[48,4096]{1,0:T(8,128)(2,1)S(1)}, u32[]{:S(2)}, u32[]{:S(2)}) collective-permute-start(bf16[48,4096]{1,0:T(8,128)(2,1)S(1)} %constant_dynamic-slice_fusion), channel_id=1, source_target_pairs={{0,8},{8,0},{1,9},{9,1},{2,10},{10,2},{3,11},{11,3},{4,12},{12,4},... | collective-permute-start | bytes 1179656 | tf_op jit(solution)/shard_map/ppermute | solution.py:57

commit v2 on v1

--- a/solution.py
+++ b/solution.py
@@ -23,16 +23,17 @@
     scales = lax.dynamic_slice_in_dim(w_scales, core * HALF_ROWS, HALF_ROWS, 0)
     mine = (codes.astype(jnp.float32) * scales[..., None]).astype(jnp.bfloat16)
     mine = mine.reshape(HALF_ROWS, SHARD)
-    mirror = [
-        (lo * Z_HI + hi, (Z_LO - 1 - lo) * Z_HI + (1 - hi))
+    shift = [
+        (lo * Z_HI + hi, (lo + Z_LO // 2) % Z_LO * Z_HI + (1 - hi))
         for lo in range(Z_LO)
         for hi in range(Z_HI)
     ]
-    other = lax.ppermute(mine, ("z_lo", "z_hi"), mirror)
+    other = lax.ppermute(mine, ("z_lo", "z_hi"), shift)
     first = jnp.where(z_hi == 0, mine, other)
     second = jnp.where(z_hi == 0, other, mine)
     both = jnp.stack([first, second])
-    return lax.all_gather(both, "x", axis=0)
+    copies = jnp.broadcast_to(both[None], (X,) + both.shape)
+    return lax.all_to_all(copies, "x", split_axis=0, concat_axis=0, tiled=True)
 
 
 def on_device(tokens, cotangent, w_codes, w_scales):
@@ -56,12 +57,13 @@
     give = lax.dynamic_slice_in_dim(local_grad, (1 - core) * width, width, 1)
     got = lax.ppermute(give, "core", swap)
     chip = (keep.astype(jnp.float32) + got.astype(jnp.float32)).astype(jnp.bfloat16)
-    by_x = chip.reshape(ROWS, Z_HI, X, PIECE).transpose(2, 0, 1, 3).reshape(X, ROWS, Z_HI * PIECE)
-    from_x = lax.all_to_all(by_x, "x", split_axis=0, concat_axis=0, tiled=True)
-    row_sum = jnp.sum(from_x.astype(jnp.float32), axis=0).astype(jnp.bfloat16)
-    by_yz = row_sum.reshape(ROWS * Z_HI, PIECE // BLOCK, BLOCK)
-    from_yz = lax.all_to_all(by_yz, ("z_lo", "y", "z_hi"), split_axis=0, concat_axis=0, tiled=True)
-    return jnp.sum(from_yz.astype(jnp.float32), axis=0)
+    by_yx = chip.reshape(Z_LO, Y, Z_HI, X, PIECE).transpose(1, 3, 0, 2, 4)
+    by_yx = by_yx.reshape(Y * X, Z_LO * Z_HI * PIECE // BLOCK, BLOCK)
+    from_yx = lax.all_to_all(by_yx, ("y", "x"), split_axis=0, concat_axis=0, tiled=True)
+    part = jnp.sum(from_yx.astype(jnp.float32), axis=0).astype(jnp.bfloat16)
+    by_z = part.reshape(Z_LO * Z_HI, PIECE // BLOCK, BLOCK)
+    from_z = lax.all_to_all(by_z, ("z_lo", "z_hi"), split_axis=0, concat_axis=0, tiled=True)
+    return jnp.sum(from_z.astype(jnp.float32), axis=0)
 
 
 def solution(mesh):

time: 89.5 us -> 89.8 us (level)
  the two profiles are of different devices: /device:TPU:1 before, /device:TPU:8 now
where the time goes in v2:
time: 89.8 us; the launch traced here: 89.4 us
  blocking collectives  53 us (59%)
  starting transfers between devices  18.5 us (21%)
  matrix products  6.41 us (7%)
  waiting for transfers between devices  5.39 us (6%)
  local copies, waits for them, and re-layouts  3.04 us (3%)
  other arithmetic  2.84 us (3%)
    all_to_all x1, blocking collectives, on_device(): lax.all_to_all(by_yx, ('y', 'x'), split_axis=0, concat_axis=0, tiled=True)  23.1 us
    all_to_all x1, blocking collectives, on_device(): lax.all_to_all(by_z, ('z_lo', 'z_hi'), split_axis=0, concat_axis=0, tiled...  18.5 us
    ppermute x1, starting transfers between devices, gather_weight(): other = lax.ppermute(mine, ('z_lo', 'z_hi'), shift)  14.6 us
    all_to_all x1, blocking collectives, gather_weight(): return lax.all_to_all(copies, 'x', split_axis=0, concat_axis=0, tiled=True)  11.5 us
    dot_general x1, matrix products, on_device(): lax.dot_general(delta, tokens, (((0,), (0,)), ((), ())), preferred_elemen...  6.41 us
    ppermute x1, waiting for transfers between devices, gather_weight(): other = lax.ppermute(mine, ('z_lo', 'z_hi'), shift)  2.15 us
    ppermute x1, starting transfers between devices, on_device(): got = lax.ppermute(give, 'core', swap)  2.04 us
    ppermute x1, starting transfers between devices, on_device(): their_rows = lax.ppermute(my_rows, 'core', swap)  1.91 us
  transfers between devices with their start and end apart: 3, of which 3 were waited for; matrix products, arithmetic and copies ran while one was open for 0% of the time, Pallas kernels for 0%

profile of v2, /device:TPU:8, one launch (start us, length us, event | category | flops | bytes accessed | tf_op | source)
XLA Modules:
  0.0 89.4 jit_solution(2397349357698127846)
XLA Ops:
  0.0 0.0 copy-start
  0.0 0.0 copy-start.1
  0.0 0.7 copy-done
  0.7 0.1 constant_dynamic-slice_fusion.1
  0.8 0.1 copy.17
  0.8 0.9 multiply_convert_fusion
  1.7 14.6 %collective-permute-start = (bf16[24,1024]{1,0:T(8,128)(2,1)S(1)}, bf16[24,1024]{1,0:T(8,128)(2,1)S(1)}, u32[]{:S(2)}, u32[]{:S(2)}) collective-permute-start(bf16[24,1024]{1,0:T(8,128)(2,1)S(1)} %bitcast.37), channel_id=1, source_target_pairs={{0,388},{4,384},{128,516},{132,512},{256,644},{260,640},{384,4},{3... | collective-permute-start | bytes 147464 | tf_op jit(solution)/shard_map/ppermute | solution.py:31
  16.3 2.1 %collective-permute-done = bf16[24,1024]{1,0:T(8,128)(2,1)S(1)} collective-permute-done((bf16[24,1024]{1,0:T(8,128)(2,1)S(1)}, bf16[24,1024]{1,0:T(8,128)(2,1)S(1)}, u32[]{:S(2)}, u32[]{:S(2)}) %collective-permute-start) | collective-permute-done | bytes 49184 | tf_op jit(solution)/shard_map/ppermute | solution.py:31
  18.5 0.1 copy.18
  18.6 0.2 broadcast_in_dim.2
  18.8 11.5 %all_to_all.15 = bf16[4,2,24,1024]{3,1,2,0:T(2,128)(2,1)S(1)} all-to-all(bf16[4,2,24,1024]{3,1,2,0:T(2,128)(2,1)S(1)} %broadcast_in_dim.2), channel_id=1, replica_groups=mesh['z_lo'=6,'y'=8,'core'=2,'z_hi'=2,'x'=4] {'x'}, dimensions={0} | all-to-all | bytes 786432 | tf_op jit(solution)/shard_map/all_to_all | solution.py:36
  30.3 1.9 %collective-permute-start.1 = (bf16[4,2,24,1024]{3,1,2,0:T(2,128)(2,1)S(1)}, bf16[4,2,24,1024]{3,1,2,0:T(2,128)(2,1)S(1)}, u32[]{:S(2)}, u32[]{:S(2)}) collective-permute-start(bf16[4,2,24,1024]{3,1,2,0:T(2,128)(2,1)S(1)} %all_to_all.15), channel_id=1, source_target_pairs={{0,8},{8,0},{1,9},{9,1},{2,10},{10,2},{3,11},{11,3},{4,12},{12,4},... | collective-permute-start | bytes 1179656 | tf_op jit(solution)/shard_map/ppermute | solution.py:43
  32.2 1.7 %collective-permute-done.1 = bf16[4,2,24,1024]{3,1,2,0:T(2,128)(2,1)S(1)} collective-permute-done((bf16[4,2,24,1024]{3,1,2,0:T(2,128)(2,1)S(1)}, bf16[4,2,24,1024]{3,1,2,0:T(2,128)(2,1)S(1)}, u32[]{:S(2)}, u32[]{:S(2)}) %collective-permute-start.1) | collective-permute-done | bytes 393248 | tf_op jit(solution)/shard_map/ppermute | solution.py:43
  33.9 1.2 %fusion = bf16[2,24,2,4,1024]{4,2,1,3,0:T(2,128)(2,1)S(1)} fusion(pred[]{:T(512)S(6)} %eq.7, bf16[1,4,2,24,1024]{4,2,3,1,0:T(2,128)(2,1)S(1)} %bitcast.35, bf16[1,4,2,24,1024]{4,2,3,1,0:T(2,128)(2,1)S(1)} %bitcast.31), kind=kLoop, calls=%fused_computation.3 | loop fusion | flops 1179648 | bytes 1572865 | tf_op jit(solution)/shard_map/transpose | solution.py:47
  35.1 0.6 copy.19
  35.7 0.6 reshape.18
  36.3 0.0 copy-done.1
  36.3 6.4 %convolution_convert_fusion = bf16[48,8192]{1,0:T(8,128)(2,1)S(1)} fusion(bf16[256,8192]{1,0:T(8,128)(2,1)} %param.4, bf16[48,8192]{1,0:T(8,128)(2,1)S(1)} %reshape.18, bf16[256,48]{0,1:T(8,128)(2,1)S(1)} %copy-done.1), kind=kOutput, calls=%fused_computation | convolution fusion | flops 403169280 | bytes 5791744 | tf_op jit(solution)/shard_map/dot_general | solution.py:52
  42.8 2.0 %collective-permute-start.2 = (bf16[48,4096]{1,0:T(8,128)(2,1)S(1)}, bf16[48,4096]{1,0:T(8,128)(2,1)S(1)}, u32[]{:S(2)}, u32[]{:S(2)}) collective-permute-start(bf16[48,4096]{1,0:T(8,128)(2,1)S(1)} %constant_dynamic-slice_fusion), channel_id=1, source_target_pairs={{0,8},{8,0},{1,9},{9,1},{2,10},{10,2},{3,11},{11,3},{4,12},{12,4},... | collective-permute-start | bytes 1179656 | tf_op jit(solution)/shard_map/ppermute | solution.py:58
  44.8 1.6 %collective-permute-done.2 = bf16[48,4096]{1,0:T(8,128)(2,1)S(1)} collective-permute-done((bf16[48,4096]{1,0:T(8,128)(2,1)S(1)}, bf16[48,4096]{1,0:T(8,128)(2,1)S(1)}, u32[]{:S(2)}, u32[]{:S(2)}) %collective-permute-start.2) | collective-permute-done | bytes 393248 | tf_op jit(solution)/shard_map/ppermute | solution.py:58
  46.4 0.1 add_convert_fusion
  46.5 0.4 copy.28
  46.9 0.3 reshape.20
  47.1 23.1 %all_to_all.16 = bf16[32,48,128]{2,1,0:T(8,128)(2,1)S(1)} all-to-all(bf16[32,48,128]{2,1,0:T(8,128)(2,1)S(1)} %reshape.20), channel_id=1, replica_groups=mesh['z_lo'=6,'y'=8,'core'=2,'z_hi'=2,'x'=4] {'y','x'}, dimensions={0} | all-to-all | bytes 786432 | tf_op jit(solution)/shard_map/all_to_all | solution.py:62
  70.3 0.1 reduce_sum.21
  70.3 18.5 %all_to_all.17 = bf16[12,4,128]{2,1,0:T(4,128)(2,1)S(1)} all-to-all(bf16[12,4,128]{2,1,0:T(4,128)(2,1)S(1)} %bitcast.36), channel_id=1, replica_groups=mesh['z_lo'=6,'y'=8,'core'=2,'z_hi'=2,'x'=4] {'z_lo','z_hi'}, dimensions={0} | all-to-all | bytes 24576 | tf_op jit(solution)/shard_map/all_to_all | solution.py:65
  88.8 0.6 convert_reduce_fusion
  (4 shorter events, 0.1 us)
Async XLA Ops:
  0.0 0.7 copy-start
  0.0 36.3 %copy-start.1 = (bf16[256,48]{0,1:T(8,128)(2,1)S(1)}, bf16[256,48]{0,1:T(8,128)(2,1)}, u32[]{:S(2)}) copy-start(bf16[256,48]{0,1:T(8,128)(2,1)} %param.5) | copy-start | bytes 73732
  1.7 16.7 %collective-permute-start = (bf16[24,1024]{1,0:T(8,128)(2,1)S(1)}, bf16[24,1024]{1,0:T(8,128)(2,1)S(1)}, u32[]{:S(2)}, u32[]{:S(2)}) collective-permute-start(bf16[24,1024]{1,0:T(8,128)(2,1)S(1)} %bitcast.37), channel_id=1, source_target_pairs={{0,388},{4,384},{128,516},{132,512},{256,644},{260,640},{384,4},{3... | collective-permute-start | bytes 147464 | tf_op jit(solution)/shard_map/ppermute | solution.py:31
  30.3 3.6 %collective-permute-start.1 = (bf16[4,2,24,1024]{3,1,2,0:T(2,128)(2,1)S(1)}, bf16[4,2,24,1024]{3,1,2,0:T(2,128)(2,1)S(1)}, u32[]{:S(2)}, u32[]{:S(2)}) collective-permute-start(bf16[4,2,24,1024]{3,1,2,0:T(2,128)(2,1)S(1)} %all_to_all.15), channel_id=1, source_target_pairs={{0,8},{8,0},{1,9},{9,1},{2,10},{10,2},{3,11},{11,3},{4,12},{12,4},... | collective-permute-start | bytes 1179656 | tf_op jit(solution)/shard_map/ppermute | solution.py:43
  42.8 3.6 %collective-permute-start.2 = (bf16[48,4096]{1,0:T(8,128)(2,1)S(1)}, bf16[48,4096]{1,0:T(8,128)(2,1)S(1)}, u32[]{:S(2)}, u32[]{:S(2)}) collective-permute-start(bf16[48,4096]{1,0:T(8,128)(2,1)S(1)} %constant_dynamic-slice_fusion), channel_id=1, source_target_pairs={{0,8},{8,0},{1,9},{9,1},{2,10},{10,2},{3,11},{11,3},{4,12},{12,4},... | collective-permute-start | bytes 1179656 | tf_op jit(solution)/shard_map/ppermute | solution.py:58

commit v3 on v2

v3 whole, which is shorter than its diff:
```python
import jax
import jax.numpy as jnp
from jax import lax
from jax.experimental import pallas as pl
from jax.experimental.pallas import tpu as pltpu
from jax.sharding import Mesh, PartitionSpec as P

BLOCK = 128
Z_LO, Y, CORE, Z_HI, X = 6, 8, 2, 2, 4
ROWS = 48
HALF_ROWS = ROWS // CORE
SHARD = 1024
PIECE = 512
PIECE_BLOCKS = PIECE // BLOCK
VMEM = pl.BlockSpec(memory_space=pltpu.VMEM)
HBM = pl.BlockSpec(memory_space=pltpu.HBM)
SMEM = pl.BlockSpec(memory_space=pltpu.SMEM)
SWAP = ((0, 1), (1, 0))


def in_vmem(array):
    return pltpu.with_memory_space_constraint(array, pltpu.VMEM)


def in_hbm(array):
    return pltpu.with_memory_space_constraint(array, pltpu.HBM)


def slope(pre):
    sig = jax.nn.sigmoid(pre)
    return sig * (1.0 + pre * (1.0 - sig))


def prepare_kernel(core_ref, codes_hbm, scales_hbm, mine_ref, codes_ref, scales_ref, sems):
    copies = [
        pltpu.make_async_copy(
            codes_hbm.at[pl.ds(core_ref[0] * HALF_ROWS, HALF_ROWS)], codes_ref, sems.at[0]
        ),
        pltpu.make_async_copy(scales_hbm, scales_ref, sems.at[1]),
    ]
    for copy in copies:
        copy.start()
    for copy in copies:
        copy.wait()
    codes = codes_ref[...].astype(jnp.float32).reshape(HALF_ROWS, SHARD)
    scales = scales_ref[...].T
    scales = jnp.where(core_ref[0] == 0, scales[:HALF_ROWS], scales[HALF_ROWS:])
    for k in range(SHARD // BLOCK):
        block = slice(k * BLOCK, (k + 1) * BLOCK)
        mine_ref[:, block] = (codes[:, block] * scales[:, k : k + 1]).astype(jnp.bfloat16)


def prepare(core, w_codes, w_scales):
    scales = w_scales.T
    return pl.pallas_call(
        prepare_kernel,
        out_shape=jax.ShapeDtypeStruct((HALF_ROWS, SHARD), jnp.bfloat16),
        in_specs=[SMEM, HBM, HBM],
        out_specs=VMEM,
        scratch_shapes=[
            pltpu.VMEM((HALF_ROWS,) + w_codes.shape[1:], w_codes.dtype),
            pltpu.VMEM(scales.shape, scales.dtype),
            pltpu.SemaphoreType.DMA((2,)),
        ],
        compiler_params=pltpu.CompilerParams(vmem_limit_bytes=8 * 2**20),
        name="prepare",
    )(core.reshape(1), in_hbm(w_codes), in_hbm(scales))


def spread_kernel(hi_ref, mine_ref, other_ref, out_ref):
    mine, other = mine_ref[...], other_ref[...]
    low = hi_ref[0] == 0
    first = jnp.where(low, mine, other)
    second = jnp.where(low, other, mine)
    for x in range(X):
        out_ref[x, :, :SHARD] = first
        out_ref[x, :, SHARD:] = second


def spread(z_hi, mine, other):
    return pl.pallas_call(
        spread_kernel,
        out_shape=jax.ShapeDtypeStruct((X, HALF_ROWS, Z_HI * SHARD), jnp.bfloat16),
        in_specs=[SMEM, VMEM, VMEM],
        out_specs=VMEM,
        compiler_params=pltpu.CompilerParams(vmem_limit_bytes=8 * 2**20),
        name="spread",
    )(z_hi.reshape(1), mine, other)


def product(w_ref, tok_ref, hi, pre):
    for x in range(X):
        rows = w_ref[x, :, pl.ds(pl.multiple_of(hi * SHARD, SHARD), SHARD)]
        columns = pl.ds(pl.multiple_of((hi * X + x) * SHARD, SHARD), SHARD)
        pre += lax.dot_general(
            rows, tok_ref[:, columns], (((1,), (1,)), ((), ())), preferred_element_type=jnp.float32
        )
    return pre


def own_kernel(w_ref, tok_hbm, pre_ref, tok_ref, sems):
    def copy(hi):
        columns = pl.ds(pl.multiple_of(hi * X * SHARD, SHARD), X * SHARD)
        return pltpu.make_async_copy(tok_hbm.at[:, columns], tok_ref.at[:, columns], sems.at[hi])

    for hi in range(Z_HI):
        copy(hi).start()

    def step(hi, pre):
        copy(hi).wait()
        return product(w_ref, tok_ref, hi, pre)

    pre_ref[...] = lax.fori_loop(0, Z_HI, step, jnp.zeros(pre_ref.shape, jnp.float32))


def own_rows(weight, tokens):
    return pl.pallas_call(
        own_kernel,
        out_shape=[
            jax.ShapeDtypeStruct((HALF_ROWS, tokens.shape[0]), jnp.float32),
            pltpu.VMEM(tokens.shape, tokens.dtype),
        ],
        in_specs=[VMEM, HBM],
        out_specs=[VMEM] * 2,
        scratch_shapes=[pltpu.SemaphoreType.DMA((Z_HI,))],
        compiler_params=pltpu.CompilerParams(vmem_limit_bytes=8 * 2**20),
        name="own_rows",
    )(weight, in_hbm(tokens))


def grad_kernel(core_ref, w_ref, pre_ref, cot_ref, tok_ref, out_ref):
    mine = pre_ref[...]
    theirs = jnp.zeros_like(mine)
    for hi in range(Z_HI):
        theirs = product(w_ref, tok_ref, hi, theirs)
    first = core_ref[0] == 0
    pre = jnp.concatenate(
        [jnp.where(first, mine, theirs), jnp.where(first, theirs, mine)], axis=0
    )
    delta = (cot_ref[...].astype(jnp.float32) * slope(pre)).astype(jnp.bfloat16)
    for h in range(CORE):
        for hi in range(Z_HI):
            for x in range(X):
                column = ((h * Z_HI + hi) * X + x) * PIECE
                out_ref[h * X + x, :, hi * PIECE : (hi + 1) * PIECE] = jnp.dot(
                    delta,
                    tok_ref[:, column : column + PIECE],
                    preferred_element_type=jnp.float32,
                ).astype(jnp.bfloat16)


def gradient(core, weight, pre, cotangent, tokens):
    return pl.pallas_call(
        grad_kernel,
        out_shape=jax.ShapeDtypeStruct((CORE * X, ROWS, Z_HI * PIECE), jnp.bfloat16),
        in_specs=[SMEM] + [VMEM] * 4,
        out_specs=VMEM,
        compiler_params=pltpu.CompilerParams(vmem_limit_bytes=8 * 2**20),
        name="gradient",
    )(core.reshape(1), weight, pre, cotangent.T, in_vmem(tokens))


def sum_kernel(in_ref, out_ref):
    total = jnp.sum(in_ref[...].astype(jnp.float32), axis=0)
    out_ref[...] = total.reshape(out_ref.shape).astype(jnp.bfloat16)


def sum_peers(parts):
    blocks = ROWS * Z_HI * PIECE_BLOCKS
    return pl.pallas_call(
        sum_kernel,
        out_shape=jax.ShapeDtypeStruct((blocks, BLOCK), jnp.bfloat16),
        in_specs=[VMEM],
        out_specs=VMEM,
        compiler_params=pltpu.CompilerParams(vmem_limit_bytes=8 * 2**20),
        name="sum_peers",
    )(parts)


def on_device(tokens, cotangent, w_codes, w_scales):
    core = lax.axis_index("core")
    z_hi = lax.axis_index("z_hi")

    mine = prepare(core, w_codes, w_scales)
    shift = [
        (lo * Z_HI + hi, (lo + Z_LO // 2) % Z_LO * Z_HI + (1 - hi))
        for lo in range(Z_LO)
        for hi in range(Z_HI)
    ]
    other = lax.ppermute(mine, ("z_lo", "z_hi"), shift)
    copies = spread(z_hi, mine, other)
    half = lax.all_to_all(copies, "x", split_axis=0, concat_axis=0, tiled=True)

    theirs = lax.ppermute(half, "core", SWAP)
    pre, staged = own_rows(half, tokens)
    grad = gradient(core, theirs, pre, cotangent, staged)

    from_x = lax.all_to_all(grad, ("core", "x"), split_axis=0, concat_axis=0, tiled=True)
    by_yz = sum_peers(from_x).reshape(Z_LO * Y * Z_HI, PIECE_BLOCKS, BLOCK)
    from_yz = lax.all_to_all(
        by_yz, ("z_lo", "y", "z_hi"), split_axis=0, concat_axis=0, tiled=True
    )
    return jnp.sum(from_yz.astype(jnp.float32), axis=0)


def solution(mesh):
    fine = Mesh(
        mesh.devices.reshape(Z_LO, Y, CORE, Z_HI, X), ("z_lo", "y", "core", "z_hi", "x")
    )
    outer, inner = ("z_lo", "y", "core"), ("z_hi", "x")
    in_specs = (
        P(outer + inner, None),
        P(outer + inner, None),
        P(None, inner, None),
        P(None, inner),
    )
    return jax.shard_map(
        on_device, mesh=fine, in_specs=in_specs, out_specs=P(outer + inner, None), check_vma=False
    )
```

time: 89.8 us -> 82.4 us (0.918)
  the two profiles are of different devices: /device:TPU:8 before, /device:TPU:1 now
where the time goes in v3:
time: 82.4 us; the launch traced here: 82 us
  blocking collectives  52.5 us (64%)
  starting transfers between devices  20 us (24%)
  Pallas kernels  7.17 us (9%)
  waiting for transfers between devices  1.58 us (2%)
    all_to_all x1, blocking collectives, on_device(): lax.all_to_all(by_yz, ('z_lo', 'y', 'z_hi'), split_axis=0, concat_axis=0,...  27.9 us
    ppermute x1, starting transfers between devices, on_device(): other = lax.ppermute(mine, ('z_lo', 'z_hi'), shift)  15.1 us
    all_to_all x1, blocking collectives, on_device(): lax.all_to_all(grad, ('core', 'x'), split_axis=0, concat_axis=0, tiled=True)  14.6 us
    all_to_all x1, blocking collectives, on_device(): half = lax.all_to_all(copies, 'x', split_axis=0, concat_axis=0, tiled=True)  10.1 us
    ppermute x1, starting transfers between devices, on_device(): theirs = lax.ppermute(half, 'core', SWAP)  4.84 us
    pallas_call x1, Pallas kernels, own_rows(): pl.pallas_call(own_kernel, out_shape=[jax.ShapeDtypeStruct((HALF_ROWS, to...  3.06 us
    pallas_call x1, Pallas kernels, gradient(): pl.pallas_call(grad_kernel, out_shape=jax.ShapeDtypeStruct((CORE * X, ROW...  2.92 us
  transfers between devices with their start and end apart: 2, of which 1 were waited for; matrix products, arithmetic and copies ran while one was open for 0% of the time, Pallas kernels for 4%

profile of v3, /device:TPU:1, one launch (start us, length us, event | category | flops | bytes accessed | tf_op | source)
XLA Modules:
  0.0 82.0 jit_solution(2509656138462678305)
XLA Ops:
  0.0 0.0 copy-start
  0.0 1.0 %prepare.1.mine_ref = bf16[24,1024]{1,0:T(8,128)(2,1)S(1)} custom-call(s32[1]{0:T(128)} %bitcast.core_ref, bf16[48,8,128]{2,1,0:T(8,128)(2,1)} %codes_hbm.1, f32[8,48]{1,0:T(8,128)} %bitcast.7), custom_call_target="tpu_custom_call" | custom-call | tf_op jit(solution)/shard_map/prepare/pallas_call | solution.py:55
  1.0 15.1 %collective-permute-start = (bf16[24,1024]{1,0:T(8,128)(2,1)S(1)}, bf16[24,1024]{1,0:T(8,128)(2,1)S(1)}, u32[]{:S(2)}, u32[]{:S(2)}) collective-permute-start(bf16[24,1024]{1,0:T(8,128)(2,1)S(1)} %prepare.1.mine_ref), channel_id=1, source_target_pairs={{0,388},{4,384},{128,516},{132,512},{256,644},{260,640},{384,4},{3... | collective-permute-start | bytes 147464 | tf_op jit(solution)/shard_map/ppermute | solution.py:190
  16.2 1.6 %collective-permute-done.other_ref = bf16[24,1024]{1,0:T(8,128)(2,1)S(1)} collective-permute-done((bf16[24,1024]{1,0:T(8,128)(2,1)S(1)}, bf16[24,1024]{1,0:T(8,128)(2,1)S(1)}, u32[]{:S(2)}, u32[]{:S(2)}) %collective-permute-start) | collective-permute-done | bytes 49184 | tf_op jit(solution)/shard_map/ppermute | solution.py:190
  17.8 10.1 %all_to_all.15.w_ref = bf16[4,24,2048]{2,1,0:T(8,128)(2,1)S(1)} all-to-all(bf16[4,24,2048]{2,1,0:T(8,128)(2,1)S(1)} %spread.1), channel_id=1, replica_groups=mesh['z_lo'=6,'y'=8,'core'=2,'z_hi'=2,'x'=4] {'x'}, dimensions={0} | all-to-all | bytes 786432 | tf_op jit(solution)/shard_map/all_to_all | solution.py:192
  27.8 4.8 %collective-permute-start.1 = (bf16[4,24,2048]{2,1,0:T(8,128)(2,1)S(1)}, bf16[4,24,2048]{2,1,0:T(8,128)(2,1)S(1)}, u32[]{:S(2)}, u32[]{:S(2)}) collective-permute-start(bf16[4,24,2048]{2,1,0:T(8,128)(2,1)S(1)} %all_to_all.15.w_ref), channel_id=1, source_target_pairs={{0,8},{8,0},{1,9},{9,1},{2,10},{10,2},{3,11},{11,3},{4,12},{12,4},... | collective-permute-start | bytes 1179656 | tf_op jit(solution)/shard_map/ppermute | solution.py:194
  32.7 3.1 %own_rows.1 = (f32[24,256]{1,0:T(8,128)S(1)}, bf16[256,8192]{1,0:T(8,128)(2,1)S(1)}) custom-call(bf16[4,24,2048]{2,1,0:T(8,128)(2,1)S(1)} %all_to_all.15.w_ref, bf16[256,8192]{1,0:T(8,128)(2,1)} %tok_hbm.1), custom_call_target="tpu_custom_call" | custom-call | tf_op jit(solution)/shard_map/own_rows/pallas_call | solution.py:117
  35.7 0.0 collective-permute-done.1.w_ref
  35.8 0.0 copy-done
  35.8 2.9 %gradient.1 = bf16[8,48,1024]{2,1,0:T(8,128)(2,1)S(1)} custom-call(s32[1]{0:T(128)} %bitcast.core_ref, bf16[4,24,2048]{2,1,0:T(8,128)(2,1)S(1)} %collective-permute-done.1.w_ref, f32[24,256]{1,0:T(8,128)S(1)} %get-tuple-element.7.pre_ref, bf16[48,256]{1,0:T(8,128)(2,1)S(1)} %bitcast.6, bf16[256,8192]{1,0:T(8,128)(2,1)S(1)} %get-tuple-element.8.tok_ref), custom_call_target="tpu_custom_call" | custom-call | tf_op jit(solution)/shard_map/gradient/pallas_call | solution.py:153
  38.7 14.6 %all_to_all.16.in_ref = bf16[8,48,1024]{2,1,0:T(8,128)(2,1)S(1)} all-to-all(bf16[8,48,1024]{2,1,0:T(8,128)(2,1)S(1)} %gradient.1), channel_id=1, replica_groups=mesh['z_lo'=6,'y'=8,'core'=2,'z_hi'=2,'x'=4] {'core','x'}, dimensions={0} | all-to-all | bytes 1572864 | tf_op jit(solution)/shard_map/all_to_all | solution.py:198
  53.3 0.1 sum_peers.1
  53.4 27.9 %all_to_all.17 = bf16[96,4,128]{2,1,0:T(4,128)(2,1)S(1)} all-to-all(bf16[96,4,128]{2,1,0:T(4,128)(2,1)S(1)} %bitcast.5), channel_id=1, replica_groups=mesh['z_lo'=6,'y'=8,'core'=2,'z_hi'=2,'x'=4] {'z_lo','y','z_hi'}, dimensions={0} | all-to-all | bytes 196608 | tf_op jit(solution)/shard_map/all_to_all | solution.py:200
  81.3 0.7 convert_reduce_fusion
  (1 shorter events, 0.0 us)
Async XLA Ops:
  0.0 35.8 %copy-start = (bf16[256,48]{0,1:T(8,128)(2,1)S(1)}, bf16[256,48]{0,1:T(8,128)(2,1)}, u32[]{:S(2)}) copy-start(bf16[256,48]{0,1:T(8,128)(2,1)} %param.5) | copy-start | bytes 73732
  1.0 16.7 %collective-permute-start = (bf16[24,1024]{1,0:T(8,128)(2,1)S(1)}, bf16[24,1024]{1,0:T(8,128)(2,1)S(1)}, u32[]{:S(2)}, u32[]{:S(2)}) collective-permute-start(bf16[24,1024]{1,0:T(8,128)(2,1)S(1)} %prepare.1.mine_ref), channel_id=1, source_target_pairs={{0,388},{4,384},{128,516},{132,512},{256,644},{260,640},{384,4},{3... | collective-permute-start | bytes 147464 | tf_op jit(solution)/shard_map/ppermute | solution.py:190
  27.8 7.9 %collective-permute-start.1 = (bf16[4,24,2048]{2,1,0:T(8,128)(2,1)S(1)}, bf16[4,24,2048]{2,1,0:T(8,128)(2,1)S(1)}, u32[]{:S(2)}, u32[]{:S(2)}) collective-permute-start(bf16[4,24,2048]{2,1,0:T(8,128)(2,1)S(1)} %all_to_all.15.w_ref), channel_id=1, source_target_pairs={{0,8},{8,0},{1,9},{9,1},{2,10},{10,2},{3,11},{11,3},{4,12},{12,4},... | collective-permute-start | bytes 1179656 | tf_op jit(solution)/shard_map/ppermute | solution.py:194

commit v4 on v3

--- a/solution.py
+++ b/solution.py
@@ -88,76 +88,157 @@
     )(z_hi.reshape(1), mine, other)
 
 
-def product(w_ref, tok_ref, hi, pre):
-    for x in range(X):
-        rows = w_ref[x, :, pl.ds(pl.multiple_of(hi * SHARD, SHARD), SHARD)]
-        columns = pl.ds(pl.multiple_of((hi * X + x) * SHARD, SHARD), SHARD)
+def stage_kernel(tok_hbm, tok_ref, sem):
+    copy = pltpu.make_async_copy(tok_hbm.at[:, : X * SHARD], tok_ref, sem)
+    copy.start()
+    copy.wait()
+
+
+def stage(tokens):
+    return pl.pallas_call(
+        stage_kernel,
+        out_shape=pltpu.VMEM((tokens.shape[0], X * SHARD), tokens.dtype),
+        in_specs=[HBM],
+        out_specs=VMEM,
+        scratch_shapes=[pltpu.SemaphoreType.DMA(())],
+        compiler_params=pltpu.CompilerParams(vmem_limit_bytes=4 * 2**20),
+        name="stage",
+    )(in_hbm(tokens))
+
+
+def product(w_ref, tok_ref, hi, first, pre):
+    for x in range(X // 2):
+        columns = pl.ds(pl.multiple_of((first + x) * SHARD, SHARD), SHARD)
         pre += lax.dot_general(
-            rows, tok_ref[:, columns], (((1,), (1,)), ((), ())), preferred_element_type=jnp.float32
+            w_ref[first + x, :, hi * SHARD : (hi + 1) * SHARD],
+            tok_ref[:, columns],
+            (((1,), (1,)), ((), ())),
+            preferred_element_type=jnp.float32,
         )
     return pre
 
 
-def own_kernel(w_ref, tok_hbm, pre_ref, tok_ref, sems):
-    def copy(hi):
-        columns = pl.ds(pl.multiple_of(hi * X * SHARD, SHARD), X * SHARD)
-        return pltpu.make_async_copy(tok_hbm.at[:, columns], tok_ref.at[:, columns], sems.at[hi])
-
-    for hi in range(Z_HI):
-        copy(hi).start()
-
-    def step(hi, pre):
-        copy(hi).wait()
-        return product(w_ref, tok_ref, hi, pre)
-
-    pre_ref[...] = lax.fori_loop(0, Z_HI, step, jnp.zeros(pre_ref.shape, jnp.float32))
-
-
-def own_rows(weight, tokens):
+def own_kernel(w_ref, low_ref, tok_hbm, pre_ref, high_ref, sems):
+    def copy(part):
+        width = X // 2 * SHARD
+        offset = pl.multiple_of(part * width, width)
+        return pltpu.make_async_copy(
+            tok_hbm.at[:, pl.ds(X * SHARD + offset, width)],
+            high_ref.at[:, pl.ds(offset, width)],
+            sems.at[part],
+        )
+
+    for part in range(2):
+        copy(part).start()
+    pre = jnp.zeros(pre_ref.shape, jnp.float32)
+    for first in (0, X // 2):
+        pre = product(w_ref, low_ref, 0, first, pre)
+
+    def step(part, pre):
+        copy(part).wait()
+        return product(w_ref, high_ref, 1, part * (X // 2), pre)
+
+    pre_ref[...] = lax.fori_loop(0, 2, step, pre)
+
+
+def own_rows(weight, low, tokens):
     return pl.pallas_call(
         own_kernel,
         out_shape=[
             jax.ShapeDtypeStruct((HALF_ROWS, tokens.shape[0]), jnp.float32),
-            pltpu.VMEM(tokens.shape, tokens.dtype),
+            pltpu.VMEM(low.shape, low.dtype),
         ],
-        in_specs=[VMEM, HBM],
+        in_specs=[VMEM, VMEM, HBM],
         out_specs=[VMEM] * 2,
-        scratch_shapes=[pltpu.SemaphoreType.DMA((Z_HI,))],
+        scratch_shapes=[pltpu.SemaphoreType.DMA((2,))],
         compiler_params=pltpu.CompilerParams(vmem_limit_bytes=8 * 2**20),
         name="own_rows",
-    )(weight, in_hbm(tokens))
-
-
-def grad_kernel(core_ref, w_ref, pre_ref, cot_ref, tok_ref, out_ref):
+    )(weight, in_vmem(low), in_hbm(tokens))
+
+
+def grad_half(delta, tok_ref, out_ref):
+    for hi in range(Z_HI):
+        for x in range(X):
+            column = (hi * X + x) * PIECE
+            out_ref[x, :, hi * PIECE : (hi + 1) * PIECE] = jnp.dot(
+                delta, tok_ref[:, column : column + PIECE], preferred_element_type=jnp.float32
+            ).astype(out_ref.dtype)
+
+
+def give_kernel(core_ref, w_ref, pre_ref, cot_ref, low_ref, high_ref, delta_ref, out_ref):
     mine = pre_ref[...]
     theirs = jnp.zeros_like(mine)
-    for hi in range(Z_HI):
-        theirs = product(w_ref, tok_ref, hi, theirs)
+    for hi, tok_ref in enumerate((low_ref, high_ref)):
+        for x in (0, X // 2):
+            theirs = product(w_ref, tok_ref, hi, x, theirs)
     first = core_ref[0] == 0
     pre = jnp.concatenate(
         [jnp.where(first, mine, theirs), jnp.where(first, theirs, mine)], axis=0
     )
     delta = (cot_ref[...].astype(jnp.float32) * slope(pre)).astype(jnp.bfloat16)
-    for h in range(CORE):
-        for hi in range(Z_HI):
-            for x in range(X):
-                column = ((h * Z_HI + hi) * X + x) * PIECE
-                out_ref[h * X + x, :, hi * PIECE : (hi + 1) * PIECE] = jnp.dot(
-                    delta,
-                    tok_ref[:, column : column + PIECE],
-                    preferred_element_type=jnp.float32,
-                ).astype(jnp.bfloat16)
-
-
-def gradient(core, weight, pre, cotangent, tokens):
-    return pl.pallas_call(
-        grad_kernel,
-        out_shape=jax.ShapeDtypeStruct((CORE * X, ROWS, Z_HI * PIECE), jnp.bfloat16),
-        in_specs=[SMEM] + [VMEM] * 4,
-        out_specs=VMEM,
-        compiler_params=pltpu.CompilerParams(vmem_limit_bytes=8 * 2**20),
-        name="gradient",
-    )(core.reshape(1), weight, pre, cotangent.T, in_vmem(tokens))
+    delta_ref[...] = delta
+
+    @pl.when(first)
+    def _():
+        grad_half(delta, high_ref, out_ref)
+
+    @pl.when(jnp.logical_not(first))
+    def _():
+        grad_half(delta, low_ref, out_ref)
+
+
+def give(core, weight, pre, cotangent, low, high):
+    cotangent = cotangent.T
+    return pl.pallas_call(
+        give_kernel,
+        out_shape=[
+            jax.ShapeDtypeStruct(cotangent.shape, jnp.bfloat16),
+            jax.ShapeDtypeStruct((X, ROWS, Z_HI * PIECE), jnp.bfloat16),
+        ],
+        in_specs=[SMEM] + [VMEM] * 5,
+        out_specs=[VMEM] * 2,
+        compiler_params=pltpu.CompilerParams(vmem_limit_bytes=8 * 2**20),
+        name="give",
+    )(core.reshape(1), weight, pre, cotangent, in_vmem(low), in_vmem(high))
+
+
+def keep_kernel(core_ref, delta_ref, low_ref, high_ref, out_ref):
+    first = core_ref[0] == 0
+    delta = delta_ref[...]
+
+    @pl.when(first)
+    def _():
+        grad_half(delta, low_ref, out_ref)
+
+    @pl.when(jnp.logical_not(first))
+    def _():
+        grad_half(delta, high_ref, out_ref)
+
+
+def keep(core, delta, low, high):
+    return pl.pallas_call(
+        keep_kernel,
+        out_shape=jax.ShapeDtypeStruct((X, ROWS, Z_HI * PIECE), jnp.float32),
+        in_specs=[SMEM] + [VMEM] * 3,
+        out_specs=VMEM,
+        compiler_params=pltpu.CompilerParams(vmem_limit_bytes=8 * 2**20),
+        name="keep",
+    )(core.reshape(1), delta, in_vmem(low), in_vmem(high))
+
+
+def add_kernel(kept_ref, got_ref, out_ref):
+    out_ref[...] = (kept_ref[...] + got_ref[...].astype(jnp.float32)).astype(jnp.bfloat16)
+
+
+def add(kept, got):
+    return pl.pallas_call(
+        add_kernel,
+        out_shape=jax.ShapeDtypeStruct(got.shape, jnp.bfloat16),
+        in_specs=[VMEM] * 2,
+        out_specs=VMEM,
+        compiler_params=pltpu.CompilerParams(vmem_limit_bytes=8 * 2**20),
+        name="add",
+    )(kept, got)
 
 
 def sum_kernel(in_ref, out_ref):
@@ -188,14 +269,20 @@
         for hi in range(Z_HI)
     ]
     other = lax.ppermute(mine, ("z_lo", "z_hi"), shift)
+    late_tokens, _ = lax.optimization_barrier((tokens, mine))
+    low = stage(late_tokens)
     copies = spread(z_hi, mine, other)
+    copies, low = lax.optimization_barrier((copies, low))
     half = lax.all_to_all(copies, "x", split_axis=0, concat_axis=0, tiled=True)
 
     theirs = lax.ppermute(half, "core", SWAP)
-    pre, staged = own_rows(half, tokens)
-    grad = gradient(core, theirs, pre, cotangent, staged)
-
-    from_x = lax.all_to_all(grad, ("core", "x"), split_axis=0, concat_axis=0, tiled=True)
+    pre, high = own_rows(half, low, tokens)
+
+    delta, given = give(core, theirs, pre, cotangent, low, high)
+    got = lax.ppermute(given, "core", SWAP)
+    kept = keep(core, delta, low, high)
+
+    from_x = lax.all_to_all(add(kept, got), "x", split_axis=0, concat_axis=0, tiled=True)
     by_yz = sum_peers(from_x).reshape(Z_LO * Y * Z_HI, PIECE_BLOCKS, BLOCK)
     from_yz = lax.all_to_all(
         by_yz, ("z_lo", "y", "z_hi"), split_axis=0, concat_axis=0, tiled=True

time: 82.4 us -> 80 us (0.971)
  blocking collectives: 52.5 us -> 48.1 us
  starting transfers between devices: 20 us -> 22 us
    all_to_all x1, blocking collectives: 14.6 us -> 10.2 us  [on_device(): lax.all_to_all(add(kept, got), 'x', split_axis=0, concat_axis=0, tiled=True)]
    ppermute x0 -> x1, starting transfers between devices: none -> 1.93 us  [on_device(): got = lax.ppermute(given, 'core', SWAP)]
    ppermute x1, waiting for transfers between devices: 1.58 us -> 0.01 us  [on_device(): other = lax.ppermute(mine, ('z_lo', 'z_hi'), shift)]
    ppermute x0 -> x1, waiting for transfers between devices: none -> 1.2 us  [on_device(): got = lax.ppermute(given, 'core', SWAP)]
    pallas_call x1 -> x4, Pallas kernels: 2.92 us -> 4.01 us  [the longest x1 1.82 us: give(): pl.pallas_call(give_kernel, out_shape=[jax.ShapeDtypeStruct(cotangent.sha...]
    pallas_call x1, Pallas kernels: 3.06 us -> 2.13 us  [own_rows(): pl.pallas_call(own_kernel, out_shape=[jax.ShapeDtypeStruct((HALF_ROWS, to...]
  transfers between devices with their start and end apart: 2 -> 3, of which waited for: 1 -> 1; matrix products, arithmetic and copies ran while one was open for 0% -> 0% of each run, Pallas kernels for 4% -> 5%
where the time goes in v4:
time: 80 us; the launch traced here: 79.3 us
  blocking collectives  48.1 us (60%)
  starting transfers between devices  22 us (28%)
  Pallas kernels  7.27 us (9%)
  waiting for transfers between devices  1.2 us (2%)
    all_to_all x1, blocking collectives, on_device(): lax.all_to_all(by_yz, ('z_lo', 'y', 'z_hi'), split_axis=0, concat_axis=0,...  27.9 us
    ppermute x1, starting transfers between devices, on_device(): other = lax.ppermute(mine, ('z_lo', 'z_hi'), shift)  15.1 us
    all_to_all x1, blocking collectives, on_device(): lax.all_to_all(add(kept, got), 'x', split_axis=0, concat_axis=0, tiled=True)  10.2 us
    all_to_all x1, blocking collectives, on_device(): half = lax.all_to_all(copies, 'x', split_axis=0, concat_axis=0, tiled=True)  10.1 us
    ppermute x1, starting transfers between devices, on_device(): theirs = lax.ppermute(half, 'core', SWAP)  4.92 us
    pallas_call x1, Pallas kernels, own_rows(): pl.pallas_call(own_kernel, out_shape=[jax.ShapeDtypeStruct((HALF_ROWS, to...  2.13 us
    ppermute x1, starting transfers between devices, on_device(): got = lax.ppermute(given, 'core', SWAP)  1.93 us
    pallas_call x1, Pallas kernels, give(): pl.pallas_call(give_kernel, out_shape=[jax.ShapeDtypeStruct(cotangent.sha...  1.82 us
  transfers between devices with their start and end apart: 3, of which 1 were waited for; matrix products, arithmetic and copies ran while one was open for 0% of the time, Pallas kernels for 5%

profile of v4, /device:TPU:1, one launch (start us, length us, event | category | flops | bytes accessed | tf_op | source)
XLA Modules:
  0.0 79.3 jit_solution(7116539527467838237)
XLA Ops:
  0.0 1.0 %prepare.1.mine_ref = bf16[24,1024]{1,0:T(8,128)(2,1)S(1)} custom-call(s32[1]{0:T(128)} %bitcast.core_ref, bf16[48,8,128]{2,1,0:T(8,128)(2,1)} %codes_hbm.1, f32[8,48]{1,0:T(8,128)} %bitcast.7), custom_call_target="tpu_custom_call" | custom-call | tf_op jit(solution)/shard_map/prepare/pallas_call | solution.py:55
  1.0 15.1 %collective-permute-start = (bf16[24,1024]{1,0:T(8,128)(2,1)S(1)}, bf16[24,1024]{1,0:T(8,128)(2,1)S(1)}, u32[]{:S(2)}, u32[]{:S(2)}) collective-permute-start(bf16[24,1024]{1,0:T(8,128)(2,1)S(1)} %prepare.1.mine_ref), channel_id=1, source_target_pairs={{0,388},{4,384},{128,516},{132,512},{256,644},{260,640},{384,4},{3... | collective-permute-start | bytes 147464 | tf_op jit(solution)/shard_map/ppermute | solution.py:271
  16.1 1.6 %stage.1.low_ref = bf16[256,4096]{1,0:T(8,128)(2,1)S(1)} custom-call(bf16[256,8192]{1,0:T(8,128)(2,1)} %tok_hbm.2), custom_call_target="tpu_custom_call" | custom-call | tf_op jit(solution)/shard_map/stage/pallas_call | solution.py:98
  17.8 0.0 collective-permute-done.other_ref
  17.8 10.1 %all_to_all.15.w_ref = bf16[4,24,2048]{2,1,0:T(8,128)(2,1)S(1)} all-to-all(bf16[4,24,2048]{2,1,0:T(8,128)(2,1)S(1)} %spread.1), channel_id=1, replica_groups=mesh['z_lo'=6,'y'=8,'core'=2,'z_hi'=2,'x'=4] {'x'}, dimensions={0} | all-to-all | bytes 786432 | tf_op jit(solution)/shard_map/all_to_all | solution.py:276
  27.9 0.0 copy-start
  27.9 4.9 %collective-permute-start.1 = (bf16[4,24,2048]{2,1,0:T(8,128)(2,1)S(1)}, bf16[4,24,2048]{2,1,0:T(8,128)(2,1)S(1)}, u32[]{:S(2)}, u32[]{:S(2)}) collective-permute-start(bf16[4,24,2048]{2,1,0:T(8,128)(2,1)S(1)} %all_to_all.15.w_ref), channel_id=1, source_target_pairs={{0,8},{8,0},{1,9},{9,1},{2,10},{10,2},{3,11},{11,3},{4,12},{12,4},... | collective-permute-start | bytes 1179656 | tf_op jit(solution)/shard_map/ppermute | solution.py:278
  32.8 2.1 %own_rows.1 = (f32[24,256]{1,0:T(8,128)S(1)}, bf16[256,4096]{1,0:T(8,128)(2,1)S(1)}) custom-call(bf16[4,24,2048]{2,1,0:T(8,128)(2,1)S(1)} %all_to_all.15.w_ref, bf16[256,4096]{1,0:T(8,128)(2,1)S(1)} %stage.1.low_ref, bf16[256,8192]{1,0:T(8,128)(2,1)} %tok_hbm.2), custom_call_target="tpu_custom_call" | custom-call | tf_op jit(solution)/shard_map/own_rows/pallas_call | solution.py:145
  34.9 0.0 collective-permute-done.1.w_ref
  34.9 0.0 copy-done
  35.0 1.8 %give.1 = (bf16[48,256]{1,0:T(8,128)(2,1)S(1)}, bf16[4,48,1024]{2,1,0:T(8,128)(2,1)S(1)}) custom-call(s32[1]{0:T(128)} %bitcast.core_ref, bf16[4,24,2048]{2,1,0:T(8,128)(2,1)S(1)} %collective-permute-done.1.w_ref, f32[24,256]{1,0:T(8,128)S(1)} %get-tuple-element.15.pre_ref, bf16[48,256]{1,0:T(8,128)(2,1)S(1)} %bitcast.6, ...), custom_call_target="tpu_custom_call" | custom-call | tf_op jit(solution)/shard_map/give/pallas_call | solution.py:192
  36.8 1.9 %collective-permute-start.2 = (bf16[4,48,1024]{2,1,0:T(8,128)(2,1)S(1)}, bf16[4,48,1024]{2,1,0:T(8,128)(2,1)S(1)}, u32[]{:S(2)}, u32[]{:S(2)}) collective-permute-start(bf16[4,48,1024]{2,1,0:T(8,128)(2,1)S(1)} %get-tuple-element.18), channel_id=1, source_target_pairs={{0,8},{8,0},{1,9},{9,1},{2,10},{10,2},{3,11},{11,3},{4,12},{12,4},... | collective-permute-start | bytes 1179656 | tf_op jit(solution)/shard_map/ppermute | solution.py:282
  38.7 0.5 keep.1.kept_ref
  39.2 1.2 %collective-permute-done.2.got_ref = bf16[4,48,1024]{2,1,0:T(8,128)(2,1)S(1)} collective-permute-done((bf16[4,48,1024]{2,1,0:T(8,128)(2,1)S(1)}, bf16[4,48,1024]{2,1,0:T(8,128)(2,1)S(1)}, u32[]{:S(2)}, u32[]{:S(2)}) %collective-permute-start.2) | collective-permute-done | bytes 393248 | tf_op jit(solution)/shard_map/ppermute | solution.py:282
  40.4 0.1 add.1
  40.5 10.2 %all_to_all.16.in_ref = bf16[4,48,1024]{2,1,0:T(8,128)(2,1)S(1)} all-to-all(bf16[4,48,1024]{2,1,0:T(8,128)(2,1)S(1)} %add.1), channel_id=1, replica_groups=mesh['z_lo'=6,'y'=8,'core'=2,'z_hi'=2,'x'=4] {'x'}, dimensions={0} | all-to-all | bytes 786432 | tf_op jit(solution)/shard_map/all_to_all | solution.py:285
  50.7 0.1 sum_peers.1
  50.8 27.9 %all_to_all.17 = bf16[96,4,128]{2,1,0:T(4,128)(2,1)S(1)} all-to-all(bf16[96,4,128]{2,1,0:T(4,128)(2,1)S(1)} %bitcast.5), channel_id=1, replica_groups=mesh['z_lo'=6,'y'=8,'core'=2,'z_hi'=2,'x'=4] {'z_lo','y','z_hi'}, dimensions={0} | all-to-all | bytes 196608 | tf_op jit(solution)/shard_map/all_to_all | solution.py:287
  78.6 0.7 convert_reduce_fusion
  (1 shorter events, 0.0 us)
Async XLA Ops:
  1.0 16.7 %collective-permute-start = (bf16[24,1024]{1,0:T(8,128)(2,1)S(1)}, bf16[24,1024]{1,0:T(8,128)(2,1)S(1)}, u32[]{:S(2)}, u32[]{:S(2)}) collective-permute-start(bf16[24,1024]{1,0:T(8,128)(2,1)S(1)} %prepare.1.mine_ref), channel_id=1, source_target_pairs={{0,388},{4,384},{128,516},{132,512},{256,644},{260,640},{384,4},{3... | collective-permute-start | bytes 147464 | tf_op jit(solution)/shard_map/ppermute | solution.py:271
  27.9 7.1 %copy-start = (bf16[256,48]{0,1:T(8,128)(2,1)S(1)}, bf16[256,48]{0,1:T(8,128)(2,1)}, u32[]{:S(2)}) copy-start(bf16[256,48]{0,1:T(8,128)(2,1)} %param.5) | copy-start | bytes 73732
  27.9 7.1 %collective-permute-start.1 = (bf16[4,24,2048]{2,1,0:T(8,128)(2,1)S(1)}, bf16[4,24,2048]{2,1,0:T(8,128)(2,1)S(1)}, u32[]{:S(2)}, u32[]{:S(2)}) collective-permute-start(bf16[4,24,2048]{2,1,0:T(8,128)(2,1)S(1)} %all_to_all.15.w_ref), channel_id=1, source_target_pairs={{0,8},{8,0},{1,9},{9,1},{2,10},{10,2},{3,11},{11,3},{4,12},{12,4},... | collective-permute-start | bytes 1179656 | tf_op jit(solution)/shard_map/ppermute | solution.py:278
  36.8 3.6 %collective-permute-start.2 = (bf16[4,48,1024]{2,1,0:T(8,128)(2,1)S(1)}, bf16[4,48,1024]{2,1,0:T(8,128)(2,1)S(1)}, u32[]{:S(2)}, u32[]{:S(2)}) collective-permute-start(bf16[4,48,1024]{2,1,0:T(8,128)(2,1)S(1)} %get-tuple-element.18), channel_id=1, source_target_pairs={{0,8},{8,0},{1,9},{9,1},{2,10},{10,2},{3,11},{11,3},{4,12},{12,4},... | collective-permute-start | bytes 1179656 | tf_op jit(solution)/shard_map/ppermute | solution.py:282

commit v5 on v4

--- a/solution.py
+++ b/solution.py
@@ -1,3 +1,5 @@
+import functools
+
 import jax
 import jax.numpy as jnp
 from jax import lax
@@ -9,6 +11,7 @@
 Z_LO, Y, CORE, Z_HI, X = 6, 8, 2, 2, 4
 ROWS = 48
 HALF_ROWS = ROWS // CORE
+STAGED = 5120
 SHARD = 1024
 PIECE = 512
 PIECE_BLOCKS = PIECE // BLOCK
@@ -88,16 +91,17 @@
     )(z_hi.reshape(1), mine, other)
 
 
-def stage_kernel(tok_hbm, tok_ref, sem):
-    copy = pltpu.make_async_copy(tok_hbm.at[:, : X * SHARD], tok_ref, sem)
+def stage_kernel(tok_hbm, tok_ref, sem, *, first):
+    width = tok_ref.shape[1]
+    copy = pltpu.make_async_copy(tok_hbm.at[:, first : first + width], tok_ref, sem)
     copy.start()
     copy.wait()
 
 
-def stage(tokens):
-    return pl.pallas_call(
-        stage_kernel,
-        out_shape=pltpu.VMEM((tokens.shape[0], X * SHARD), tokens.dtype),
+def stage(tokens, first, width):
+    return pl.pallas_call(
+        functools.partial(stage_kernel, first=first),
+        out_shape=pltpu.VMEM((tokens.shape[0], width), tokens.dtype),
         in_specs=[HBM],
         out_specs=VMEM,
         scratch_shapes=[pltpu.SemaphoreType.DMA(())],
@@ -106,71 +110,37 @@
     )(in_hbm(tokens))
 
 
-def product(w_ref, tok_ref, hi, first, pre):
-    for x in range(X // 2):
-        columns = pl.ds(pl.multiple_of((first + x) * SHARD, SHARD), SHARD)
-        pre += lax.dot_general(
-            w_ref[first + x, :, hi * SHARD : (hi + 1) * SHARD],
-            tok_ref[:, columns],
-            (((1,), (1,)), ((), ())),
-            preferred_element_type=jnp.float32,
-        )
-    return pre
-
-
-def own_kernel(w_ref, low_ref, tok_hbm, pre_ref, high_ref, sems):
-    def copy(part):
-        width = X // 2 * SHARD
-        offset = pl.multiple_of(part * width, width)
-        return pltpu.make_async_copy(
-            tok_hbm.at[:, pl.ds(X * SHARD + offset, width)],
-            high_ref.at[:, pl.ds(offset, width)],
-            sems.at[part],
-        )
-
-    for part in range(2):
-        copy(part).start()
-    pre = jnp.zeros(pre_ref.shape, jnp.float32)
-    for first in (0, X // 2):
-        pre = product(w_ref, low_ref, 0, first, pre)
-
-    def step(part, pre):
-        copy(part).wait()
-        return product(w_ref, high_ref, 1, part * (X // 2), pre)
-
-    pre_ref[...] = lax.fori_loop(0, 2, step, pre)
-
-
-def own_rows(weight, low, tokens):
-    return pl.pallas_call(
-        own_kernel,
-        out_shape=[
-            jax.ShapeDtypeStruct((HALF_ROWS, tokens.shape[0]), jnp.float32),
-            pltpu.VMEM(low.shape, low.dtype),
-        ],
-        in_specs=[VMEM, VMEM, HBM],
-        out_specs=[VMEM] * 2,
-        scratch_shapes=[pltpu.SemaphoreType.DMA((2,))],
-        compiler_params=pltpu.CompilerParams(vmem_limit_bytes=8 * 2**20),
-        name="own_rows",
-    )(weight, in_vmem(low), in_hbm(tokens))
-
-
-def grad_half(delta, tok_ref, out_ref):
+def columns_of(low_ref, high_ref, first, width):
+    if first < low_ref.shape[1]:
+        return low_ref[:, first : first + width]
+    first -= low_ref.shape[1]
+    return high_ref[:, first : first + width]
+
+
+def grad_half(delta, low_ref, high_ref, core, out_ref):
     for hi in range(Z_HI):
         for x in range(X):
-            column = (hi * X + x) * PIECE
+            column = ((core * Z_HI + hi) * X + x) * PIECE
             out_ref[x, :, hi * PIECE : (hi + 1) * PIECE] = jnp.dot(
-                delta, tok_ref[:, column : column + PIECE], preferred_element_type=jnp.float32
+                delta,
+                columns_of(low_ref, high_ref, column, PIECE),
+                preferred_element_type=jnp.float32,
             ).astype(out_ref.dtype)
 
 
-def give_kernel(core_ref, w_ref, pre_ref, cot_ref, low_ref, high_ref, delta_ref, out_ref):
-    mine = pre_ref[...]
-    theirs = jnp.zeros_like(mine)
-    for hi, tok_ref in enumerate((low_ref, high_ref)):
-        for x in (0, X // 2):
-            theirs = product(w_ref, tok_ref, hi, x, theirs)
+def give_kernel(core_ref, mine_ref, theirs_ref, cot_ref, low_ref, high_ref, delta_ref, out_ref):
+    pre = jnp.zeros((ROWS, cot_ref.shape[1]), jnp.float32)
+    for hi in range(Z_HI):
+        for x in range(X):
+            part = slice(hi * SHARD, (hi + 1) * SHARD)
+            rows = jnp.concatenate([mine_ref[x, :, part], theirs_ref[x, :, part]], axis=0)
+            pre += lax.dot_general(
+                rows,
+                columns_of(low_ref, high_ref, (hi * X + x) * SHARD, SHARD),
+                (((1,), (1,)), ((), ())),
+                preferred_element_type=jnp.float32,
+            )
+    mine, theirs = pre[:HALF_ROWS], pre[HALF_ROWS:]
     first = core_ref[0] == 0
     pre = jnp.concatenate(
         [jnp.where(first, mine, theirs), jnp.where(first, theirs, mine)], axis=0
@@ -180,14 +150,14 @@
 
     @pl.when(first)
     def _():
-        grad_half(delta, high_ref, out_ref)
+        grad_half(delta, low_ref, high_ref, 1, out_ref)
 
     @pl.when(jnp.logical_not(first))
     def _():
-        grad_half(delta, low_ref, out_ref)
-
-
-def give(core, weight, pre, cotangent, low, high):
+        grad_half(delta, low_ref, high_ref, 0, out_ref)
+
+
+def give(core, mine, theirs, cotangent, low, high):
     cotangent = cotangent.T
     return pl.pallas_call(
         give_kernel,
@@ -199,7 +169,7 @@
         out_specs=[VMEM] * 2,
         compiler_params=pltpu.CompilerParams(vmem_limit_bytes=8 * 2**20),
         name="give",
-    )(core.reshape(1), weight, pre, cotangent, in_vmem(low), in_vmem(high))
+    )(core.reshape(1), mine, theirs, cotangent, in_vmem(low), in_vmem(high))
 
 
 def keep_kernel(core_ref, delta_ref, low_ref, high_ref, out_ref):
@@ -208,11 +178,11 @@
 
     @pl.when(first)
     def _():
-        grad_half(delta, low_ref, out_ref)
+        grad_half(delta, low_ref, high_ref, 0, out_ref)
 
     @pl.when(jnp.logical_not(first))
     def _():
-        grad_half(delta, high_ref, out_ref)
+        grad_half(delta, low_ref, high_ref, 1, out_ref)
 
 
 def keep(core, delta, low, high):
@@ -256,6 +226,23 @@
         compiler_params=pltpu.CompilerParams(vmem_limit_bytes=8 * 2**20),
         name="sum_peers",
     )(parts)
+
+
+def final_kernel(in_ref, out_ref):
+    pairs = in_ref[...].astype(jnp.float32).reshape(-1, 2 * PIECE_BLOCKS, BLOCK)
+    pair = jnp.sum(pairs, axis=0)
+    out_ref[...] = pair[:PIECE_BLOCKS] + pair[PIECE_BLOCKS:]
+
+
+def final_sum(parts):
+    return pl.pallas_call(
+        final_kernel,
+        out_shape=jax.ShapeDtypeStruct(parts.shape[1:], jnp.float32),
+        in_specs=[VMEM],
+        out_specs=VMEM,
+        compiler_params=pltpu.CompilerParams(vmem_limit_bytes=8 * 2**20),
+        name="final_sum",
+    )(parts.reshape(-1, BLOCK))
 
 
 def on_device(tokens, cotangent, w_codes, w_scales):
@@ -270,15 +257,16 @@
     ]
     other = lax.ppermute(mine, ("z_lo", "z_hi"), shift)
     late_tokens, _ = lax.optimization_barrier((tokens, mine))
-    low = stage(late_tokens)
+    low = stage(late_tokens, 0, STAGED)
     copies = spread(z_hi, mine, other)
     copies, low = lax.optimization_barrier((copies, low))
     half = lax.all_to_all(copies, "x", split_axis=0, concat_axis=0, tiled=True)
 
     theirs = lax.ppermute(half, "core", SWAP)
-    pre, high = own_rows(half, low, tokens)
-
-    delta, given = give(core, theirs, pre, cotangent, low, high)
+    late_tokens, _ = lax.optimization_barrier((tokens, half))
+    high = stage(late_tokens, STAGED, tokens.shape[1] - STAGED)
+
+    delta, given = give(core, half, theirs, cotangent, low, high)
     got = lax.ppermute(given, "core", SWAP)
     kept = keep(core, delta, low, high)
 
@@ -287,7 +275,7 @@
     from_yz = lax.all_to_all(
         by_yz, ("z_lo", "y", "z_hi"), split_axis=0, concat_axis=0, tiled=True
     )
-    return jnp.sum(from_yz.astype(jnp.float32), axis=0)
+    return final_sum(from_yz)
 
 
 def solution(mesh):

time: 80 us -> 79.7 us (level)
    pallas_call x2 -> x3, Pallas kernels: 3.73 us -> 3.8 us  [the longest x2 3.17 us: stage(): pl.pallas_call(functools.partial(stage_kernel, first=first), out_shape=pl...]
where the time goes in v5:
time: 79.7 us; the launch traced here: 78.7 us
  blocking collectives  48.2 us (60%)
  starting transfers between devices  22.1 us (28%)
  Pallas kernels  7.36 us (9%)
  waiting for transfers between devices  0.96 us (1%)
    all_to_all x1, blocking collectives, on_device(): lax.all_to_all(by_yz, ('z_lo', 'y', 'z_hi'), split_axis=0, concat_axis=0,...  27.8 us
    ppermute x1, starting transfers between devices, on_device(): other = lax.ppermute(mine, ('z_lo', 'z_hi'), shift)  15.1 us
    all_to_all x1, blocking collectives, on_device(): lax.all_to_all(add(kept, got), 'x', split_axis=0, concat_axis=0, tiled=True)  10.3 us
    all_to_all x1, blocking collectives, on_device(): half = lax.all_to_all(copies, 'x', split_axis=0, concat_axis=0, tiled=True)  10.1 us
    ppermute x1, starting transfers between devices, on_device(): theirs = lax.ppermute(half, 'core', SWAP)  4.79 us
    pallas_call x2, Pallas kernels, stage(): pl.pallas_call(functools.partial(stage_kernel, first=first), out_shape=pl...  3.17 us
    ppermute x1, starting transfers between devices, on_device(): got = lax.ppermute(given, 'core', SWAP)  2.17 us
    pallas_call x1, Pallas kernels, give(): pl.pallas_call(give_kernel, out_shape=[jax.ShapeDtypeStruct(cotangent.sha...  1.88 us
  transfers between devices with their start and end apart: 3, of which 1 were waited for; matrix products, arithmetic and copies ran while one was open for 0% of the time, Pallas kernels for 5%

profile of v5, /device:TPU:1, one launch (start us, length us, event | category | flops | bytes accessed | tf_op | source)
XLA Modules:
  0.0 78.7 jit_solution(17801933525651366095)
XLA Ops:
  0.0 1.0 %prepare.1.mine_ref = bf16[24,1024]{1,0:T(8,128)(2,1)S(1)} custom-call(s32[1]{0:T(128)} %bitcast.core_ref, bf16[48,8,128]{2,1,0:T(8,128)(2,1)} %codes_hbm.1, f32[8,48]{1,0:T(8,128)} %bitcast.9), custom_call_target="tpu_custom_call" | custom-call | tf_op jit(solution)/shard_map/prepare/pallas_call | solution.py:58
  1.0 15.1 %collective-permute-start = (bf16[24,1024]{1,0:T(8,128)(2,1)S(1)}, bf16[24,1024]{1,0:T(8,128)(2,1)S(1)}, u32[]{:S(2)}, u32[]{:S(2)}) collective-permute-start(bf16[24,1024]{1,0:T(8,128)(2,1)S(1)} %prepare.1.mine_ref), channel_id=1, source_target_pairs={{0,388},{4,384},{128,516},{132,512},{256,644},{260,640},{384,4},{3... | collective-permute-start | bytes 147464 | tf_op jit(solution)/shard_map/ppermute | solution.py:258
  16.1 1.8 %stage.2.low_ref = bf16[256,5120]{1,0:T(8,128)(2,1)S(1)} custom-call(bf16[256,8192]{1,0:T(8,128)(2,1)} %tok_hbm.1), custom_call_target="tpu_custom_call" | custom-call | tf_op jit(solution)/shard_map/stage/pallas_call | solution.py:102
  17.9 0.0 collective-permute-done.other_ref
  18.0 10.1 %all_to_all.15.mine_ref = bf16[4,24,2048]{2,1,0:T(8,128)(2,1)S(1)} all-to-all(bf16[4,24,2048]{2,1,0:T(8,128)(2,1)S(1)} %spread.1), channel_id=1, replica_groups=mesh['z_lo'=6,'y'=8,'core'=2,'z_hi'=2,'x'=4] {'x'}, dimensions={0} | all-to-all | bytes 786432 | tf_op jit(solution)/shard_map/all_to_all | solution.py:263
  28.0 0.0 copy-start
  28.0 4.8 %collective-permute-start.1 = (bf16[4,24,2048]{2,1,0:T(8,128)(2,1)S(1)}, bf16[4,24,2048]{2,1,0:T(8,128)(2,1)S(1)}, u32[]{:S(2)}, u32[]{:S(2)}) collective-permute-start(bf16[4,24,2048]{2,1,0:T(8,128)(2,1)S(1)} %all_to_all.15.mine_ref), channel_id=1, source_target_pairs={{0,8},{8,0},{1,9},{9,1},{2,10},{10,2},{3,11},{11,3},{4,12},{12,4},... | collective-permute-start | bytes 1179656 | tf_op jit(solution)/shard_map/ppermute | solution.py:265
  32.8 1.4 %stage.3.high_ref = bf16[256,3072]{1,0:T(8,128)(2,1)S(1)} custom-call(bf16[256,8192]{1,0:T(8,128)(2,1)} %tok_hbm.1), custom_call_target="tpu_custom_call" | custom-call | tf_op jit(solution)/shard_map/stage/pallas_call | solution.py:102
  34.3 0.0 collective-permute-done.1.theirs_ref
  34.3 0.0 copy-done
  34.3 1.9 %give.1 = (bf16[48,256]{1,0:T(8,128)(2,1)S(1)}, bf16[4,48,1024]{2,1,0:T(8,128)(2,1)S(1)}) custom-call(s32[1]{0:T(128)} %bitcast.core_ref, bf16[4,24,2048]{2,1,0:T(8,128)(2,1)S(1)} %all_to_all.15.mine_ref, bf16[4,24,2048]{2,1,0:T(8,128)(2,1)S(1)} %collective-permute-done.1.theirs_ref, bf16[48,256]{1,0:T(8,128)(2,1)S(1)} %bitcast.8, ...), custom_call_target="tpu_custom_call" | custom-call | tf_op jit(solution)/shard_map/give/pallas_call | solution.py:162
  36.2 2.2 %collective-permute-start.2 = (bf16[4,48,1024]{2,1,0:T(8,128)(2,1)S(1)}, bf16[4,48,1024]{2,1,0:T(8,128)(2,1)S(1)}, u32[]{:S(2)}, u32[]{:S(2)}) collective-permute-start(bf16[4,48,1024]{2,1,0:T(8,128)(2,1)S(1)} %get-tuple-element.16), channel_id=1, source_target_pairs={{0,8},{8,0},{1,9},{9,1},{2,10},{10,2},{3,11},{11,3},{4,12},{12,4},... | collective-permute-start | bytes 1179656 | tf_op jit(solution)/shard_map/ppermute | solution.py:270
  38.3 0.5 keep.1.kept_ref
  38.8 1.0 %collective-permute-done.2.got_ref = bf16[4,48,1024]{2,1,0:T(8,128)(2,1)S(1)} collective-permute-done((bf16[4,48,1024]{2,1,0:T(8,128)(2,1)S(1)}, bf16[4,48,1024]{2,1,0:T(8,128)(2,1)S(1)}, u32[]{:S(2)}, u32[]{:S(2)}) %collective-permute-start.2) | collective-permute-done | bytes 393248 | tf_op jit(solution)/shard_map/ppermute | solution.py:270
  39.8 0.1 add.1
  39.9 10.3 %all_to_all.16.in_ref = bf16[4,48,1024]{2,1,0:T(8,128)(2,1)S(1)} all-to-all(bf16[4,48,1024]{2,1,0:T(8,128)(2,1)S(1)} %add.1), channel_id=1, replica_groups=mesh['z_lo'=6,'y'=8,'core'=2,'z_hi'=2,'x'=4] {'x'}, dimensions={0} | all-to-all | bytes 786432 | tf_op jit(solution)/shard_map/all_to_all | solution.py:273
  50.2 0.1 sum_peers.1
  50.2 27.8 %all_to_all.17 = bf16[96,4,128]{2,1,0:T(4,128)(2,1)S(1)} all-to-all(bf16[96,4,128]{2,1,0:T(4,128)(2,1)S(1)} %bitcast.7), channel_id=1, replica_groups=mesh['z_lo'=6,'y'=8,'core'=2,'z_hi'=2,'x'=4] {'z_lo','y','z_hi'}, dimensions={0} | all-to-all | bytes 196608 | tf_op jit(solution)/shard_map/all_to_all | solution.py:275
  78.1 0.6 final_sum.1
  (1 shorter events, 0.0 us)
Async XLA Ops:
  1.0 16.9 %collective-permute-start = (bf16[24,1024]{1,0:T(8,128)(2,1)S(1)}, bf16[24,1024]{1,0:T(8,128)(2,1)S(1)}, u32[]{:S(2)}, u32[]{:S(2)}) collective-permute-start(bf16[24,1024]{1,0:T(8,128)(2,1)S(1)} %prepare.1.mine_ref), channel_id=1, source_target_pairs={{0,388},{4,384},{128,516},{132,512},{256,644},{260,640},{384,4},{3... | collective-permute-start | bytes 147464 | tf_op jit(solution)/shard_map/ppermute | solution.py:258
  28.0 6.2 %copy-start = (bf16[256,48]{0,1:T(8,128)(2,1)S(1)}, bf16[256,48]{0,1:T(8,128)(2,1)}, u32[]{:S(2)}) copy-start(bf16[256,48]{0,1:T(8,128)(2,1)} %param.5) | copy-start | bytes 73732
  28.0 6.2 %collective-permute-start.1 = (bf16[4,24,2048]{2,1,0:T(8,128)(2,1)S(1)}, bf16[4,24,2048]{2,1,0:T(8,128)(2,1)S(1)}, u32[]{:S(2)}, u32[]{:S(2)}) collective-permute-start(bf16[4,24,2048]{2,1,0:T(8,128)(2,1)S(1)} %all_to_all.15.mine_ref), channel_id=1, source_target_pairs={{0,8},{8,0},{1,9},{9,1},{2,10},{10,2},{3,11},{11,3},{4,12},{12,4},... | collective-permute-start | bytes 1179656 | tf_op jit(solution)/shard_map/ppermute | solution.py:265
  36.2 3.6 %collective-permute-start.2 = (bf16[4,48,1024]{2,1,0:T(8,128)(2,1)S(1)}, bf16[4,48,1024]{2,1,0:T(8,128)(2,1)S(1)}, u32[]{:S(2)}, u32[]{:S(2)}) collective-permute-start(bf16[4,48,1024]{2,1,0:T(8,128)(2,1)S(1)} %get-tuple-element.16), channel_id=1, source_target_pairs={{0,8},{8,0},{1,9},{9,1},{2,10},{10,2},{3,11},{11,3},{4,12},{12,4},... | collective-permute-start | bytes 1179656 | tf_op jit(solution)/shard_map/ppermute | solution.py:270

commit v6 on v5

--- a/solution.py
+++ b/solution.py
@@ -8,7 +8,7 @@
 from jax.sharding import Mesh, PartitionSpec as P
 
 BLOCK = 128
-Z_LO, Y, CORE, Z_HI, X = 6, 8, 2, 2, 4
+Z_LO, Y_HI, Y_LO, CORE, Z_HI, X = 6, 4, 2, 2, 2, 4
 ROWS = 48
 HALF_ROWS = ROWS // CORE
 STAGED = 5120
@@ -34,10 +34,10 @@
     return sig * (1.0 + pre * (1.0 - sig))
 
 
-def prepare_kernel(core_ref, codes_hbm, scales_hbm, mine_ref, codes_ref, scales_ref, sems):
+def prepare_kernel(core_ref, codes_hbm, scales_hbm, mine_ref, codes_ref, scales_ref, turned_ref, sems):
     copies = [
         pltpu.make_async_copy(
-            codes_hbm.at[pl.ds(core_ref[0] * HALF_ROWS, HALF_ROWS)], codes_ref, sems.at[0]
+            codes_hbm.at[:, core_ref[0]], codes_ref, sems.at[0]
         ),
         pltpu.make_async_copy(scales_hbm, scales_ref, sems.at[1]),
     ]
@@ -46,14 +46,17 @@
     for copy in copies:
         copy.wait()
     codes = codes_ref[...].astype(jnp.float32).reshape(HALF_ROWS, SHARD)
-    scales = scales_ref[...].T
-    scales = jnp.where(core_ref[0] == 0, scales[:HALF_ROWS], scales[HALF_ROWS:])
-    for k in range(SHARD // BLOCK):
+    count = SHARD // BLOCK
+    turned_ref[:, :count] = scales_ref[...].T
+    even, odd = (turned_ref[pl.ds(y, HALF_ROWS, stride=Y_LO), :] for y in range(Y_LO))
+    scales = jnp.where(core_ref[0] == 0, even, odd)
+    for k in range(count):
         block = slice(k * BLOCK, (k + 1) * BLOCK)
         mine_ref[:, block] = (codes[:, block] * scales[:, k : k + 1]).astype(jnp.bfloat16)
 
 
 def prepare(core, w_codes, w_scales):
+    w_codes = w_codes.reshape((HALF_ROWS, Y_LO) + w_codes.shape[1:])
     scales = w_scales.T
     return pl.pallas_call(
         prepare_kernel,
@@ -61,8 +64,9 @@
         in_specs=[SMEM, HBM, HBM],
         out_specs=VMEM,
         scratch_shapes=[
-            pltpu.VMEM((HALF_ROWS,) + w_codes.shape[1:], w_codes.dtype),
+            pltpu.VMEM((HALF_ROWS,) + w_codes.shape[2:], w_codes.dtype),
             pltpu.VMEM(scales.shape, scales.dtype),
+            pltpu.VMEM((ROWS, BLOCK), scales.dtype),
             pltpu.SemaphoreType.DMA((2,)),
         ],
         compiler_params=pltpu.CompilerParams(vmem_limit_bytes=8 * 2**20),
@@ -121,11 +125,15 @@
     for hi in range(Z_HI):
         for x in range(X):
             column = ((core * Z_HI + hi) * X + x) * PIECE
-            out_ref[x, :, hi * PIECE : (hi + 1) * PIECE] = jnp.dot(
+            grad = jnp.dot(
                 delta,
                 columns_of(low_ref, high_ref, column, PIECE),
                 preferred_element_type=jnp.float32,
-            ).astype(out_ref.dtype)
+            )
+            for y in range(Y_LO):
+                out_ref[y * X + x, :, hi * PIECE : (hi + 1) * PIECE] = grad[
+                    y * HALF_ROWS : (y + 1) * HALF_ROWS
+                ].astype(out_ref.dtype)
 
 
 def give_kernel(core_ref, mine_ref, theirs_ref, cot_ref, low_ref, high_ref, delta_ref, out_ref):
@@ -158,12 +166,11 @@
 
 
 def give(core, mine, theirs, cotangent, low, high):
-    cotangent = cotangent.T
     return pl.pallas_call(
         give_kernel,
         out_shape=[
             jax.ShapeDtypeStruct(cotangent.shape, jnp.bfloat16),
-            jax.ShapeDtypeStruct((X, ROWS, Z_HI * PIECE), jnp.bfloat16),
+            jax.ShapeDtypeStruct((Y_LO * X, HALF_ROWS, Z_HI * PIECE), jnp.bfloat16),
         ],
         in_specs=[SMEM] + [VMEM] * 5,
         out_specs=[VMEM] * 2,
@@ -188,7 +195,7 @@
 def keep(core, delta, low, high):
     return pl.pallas_call(
         keep_kernel,
-        out_shape=jax.ShapeDtypeStruct((X, ROWS, Z_HI * PIECE), jnp.float32),
+        out_shape=jax.ShapeDtypeStruct((Y_LO * X, HALF_ROWS, Z_HI * PIECE), jnp.float32),
         in_specs=[SMEM] + [VMEM] * 3,
         out_specs=VMEM,
         compiler_params=pltpu.CompilerParams(vmem_limit_bytes=8 * 2**20),
@@ -217,7 +224,7 @@
 
 
 def sum_peers(parts):
-    blocks = ROWS * Z_HI * PIECE_BLOCKS
+    blocks = HALF_ROWS * Z_HI * PIECE_BLOCKS
     return pl.pallas_call(
         sum_kernel,
         out_shape=jax.ShapeDtypeStruct((blocks, BLOCK), jnp.bfloat16),
@@ -256,33 +263,37 @@
         for hi in range(Z_HI)
     ]
     other = lax.ppermute(mine, ("z_lo", "z_hi"), shift)
-    late_tokens, _ = lax.optimization_barrier((tokens, mine))
+    late_tokens, cotangent, _ = lax.optimization_barrier((tokens, cotangent, mine))
     low = stage(late_tokens, 0, STAGED)
+    cot = cotangent.T.reshape(HALF_ROWS, Y_LO, -1).transpose(1, 0, 2).reshape(ROWS, -1)
     copies = spread(z_hi, mine, other)
-    copies, low = lax.optimization_barrier((copies, low))
+    copies, low, cot = lax.optimization_barrier((copies, low, cot))
     half = lax.all_to_all(copies, "x", split_axis=0, concat_axis=0, tiled=True)
 
     theirs = lax.ppermute(half, "core", SWAP)
     late_tokens, _ = lax.optimization_barrier((tokens, half))
     high = stage(late_tokens, STAGED, tokens.shape[1] - STAGED)
 
-    delta, given = give(core, half, theirs, cotangent, low, high)
+    delta, given = give(core, half, theirs, cot, low, high)
     got = lax.ppermute(given, "core", SWAP)
     kept = keep(core, delta, low, high)
 
-    from_x = lax.all_to_all(add(kept, got), "x", split_axis=0, concat_axis=0, tiled=True)
-    by_yz = sum_peers(from_x).reshape(Z_LO * Y * Z_HI, PIECE_BLOCKS, BLOCK)
+    from_x = lax.all_to_all(
+        add(kept, got), ("y_lo", "x"), split_axis=0, concat_axis=0, tiled=True
+    )
+    by_yz = sum_peers(from_x).reshape(Z_LO * Y_HI * Z_HI, PIECE_BLOCKS, BLOCK)
     from_yz = lax.all_to_all(
-        by_yz, ("z_lo", "y", "z_hi"), split_axis=0, concat_axis=0, tiled=True
+        by_yz, ("z_lo", "y_hi", "z_hi"), split_axis=0, concat_axis=0, tiled=True
     )
     return final_sum(from_yz)
 
 
 def solution(mesh):
     fine = Mesh(
-        mesh.devices.reshape(Z_LO, Y, CORE, Z_HI, X), ("z_lo", "y", "core", "z_hi", "x")
-    )
-    outer, inner = ("z_lo", "y", "core"), ("z_hi", "x")
+        mesh.devices.reshape(Z_LO, Y_HI, Y_LO, CORE, Z_HI, X),
+        ("z_lo", "y_hi", "y_lo", "core", "z_hi", "x"),
+    )
+    outer, inner = ("z_lo", "y_hi", "y_lo", "core"), ("z_hi", "x")
     in_specs = (
         P(outer + inner, None),
         P(outer + inner, None),

time: 79.7 us -> 79.1 us (level)
  blocking collectives: 48.2 us -> 47.1 us
    all_to_all x2, blocking collectives: 38.1 us -> 36.7 us  [the longest x1 25.8 us: on_device(): lax.all_to_all(by_yz, ('z_lo', 'y_hi', 'z_hi'), split_axis=0, concat_axis...]
  transfers between devices with their start and end apart: 3 -> 3, of which waited for: 1 -> 1; matrix products, arithmetic and copies ran while one was open for 0% -> 1% of each run, Pallas kernels for 5% -> 5%
where the time goes in v6:
time: 79.1 us; the launch traced here: 77.9 us
  blocking collectives  47.1 us (60%)
  starting transfers between devices  21.6 us (27%)
  Pallas kernels  7.32 us (9%)
  waiting for transfers between devices  0.96 us (1%)
    all_to_all x1, blocking collectives, on_device(): lax.all_to_all(by_yz, ('z_lo', 'y_hi', 'z_hi'), split_axis=0, concat_axis...  25.8 us
    ppermute x1, starting transfers between devices, on_device(): other = lax.ppermute(mine, ('z_lo', 'z_hi'), shift)  15.1 us
    all_to_all x1, blocking collectives, on_device(): lax.all_to_all(add(kept, got), ('y_lo', 'x'), split_axis=0, concat_axis=0...  10.9 us
    all_to_all x1, blocking collectives, on_device(): half = lax.all_to_all(copies, 'x', split_axis=0, concat_axis=0, tiled=True)  10.4 us
    ppermute x1, starting transfers between devices, on_device(): theirs = lax.ppermute(half, 'core', SWAP)  4.35 us
    pallas_call x2, Pallas kernels, stage(): pl.pallas_call(functools.partial(stage_kernel, first=first), out_shape=pl...  3.17 us
    ppermute x1, starting transfers between devices, on_device(): got = lax.ppermute(given, 'core', SWAP)  2.18 us
    pallas_call x1, Pallas kernels, give(): pl.pallas_call(give_kernel, out_shape=[jax.ShapeDtypeStruct(cotangent.sha...  1.88 us
  transfers between devices with their start and end apart: 3, of which 1 were waited for; matrix products, arithmetic and copies ran while one was open for 1% of the time, Pallas kernels for 5%

profile of v6, /device:TPU:1, one launch (start us, length us, event | category | flops | bytes accessed | tf_op | source)
XLA Modules:
  0.0 77.9 jit_solution(9865271442492059227)
XLA Ops:
  0.0 1.0 %prepare.1.mine_ref = bf16[24,1024]{1,0:T(8,128)(2,1)S(1)} custom-call(s32[1]{0:T(128)} %bitcast.core_ref, bf16[24,2,8,128]{3,2,1,0:T(8,128)(2,1)} %bitcast.13, f32[8,48]{1,0:T(8,128)} %bitcast.15), custom_call_target="tpu_custom_call" | custom-call | tf_op jit(solution)/shard_map/prepare/pallas_call | solution.py:61
  1.0 15.1 %collective-permute-start = (bf16[24,1024]{1,0:T(8,128)(2,1)S(1)}, bf16[24,1024]{1,0:T(8,128)(2,1)S(1)}, u32[]{:S(2)}, u32[]{:S(2)}) collective-permute-start(bf16[24,1024]{1,0:T(8,128)(2,1)S(1)} %prepare.1.mine_ref), channel_id=1, source_target_pairs={{0,388},{4,384},{128,516},{132,512},{256,644},{260,640},{384,4},{3... | collective-permute-start | bytes 147464 | tf_op jit(solution)/shard_map/ppermute | solution.py:265
  16.2 0.8 reshape.26
  16.9 1.8 %stage.2.low_ref = bf16[256,5120]{1,0:T(8,128)(2,1)S(1)} custom-call(bf16[256,8192]{1,0:T(8,128)(2,1)} %tok_hbm.1), custom_call_target="tpu_custom_call" | custom-call | tf_op jit(solution)/shard_map/stage/pallas_call | solution.py:106
  18.7 0.0 collective-permute-done.other_ref
  18.7 10.4 %all_to_all.15.mine_ref = bf16[4,24,2048]{2,1,0:T(8,128)(2,1)S(1)} all-to-all(bf16[4,24,2048]{2,1,0:T(8,128)(2,1)S(1)} %spread.1), channel_id=1, replica_groups=mesh['z_lo'=6,'y_hi'=4,'y_lo'=2,'core'=2,'z_hi'=2,'x'=4] {'x'}, dimensions={0} | all-to-all | bytes 786432 | tf_op jit(solution)/shard_map/all_to_all | solution.py:271
  29.1 4.3 %collective-permute-start.1 = (bf16[4,24,2048]{2,1,0:T(8,128)(2,1)S(1)}, bf16[4,24,2048]{2,1,0:T(8,128)(2,1)S(1)}, u32[]{:S(2)}, u32[]{:S(2)}) collective-permute-start(bf16[4,24,2048]{2,1,0:T(8,128)(2,1)S(1)} %all_to_all.15.mine_ref), channel_id=1, source_target_pairs={{0,8},{8,0},{1,9},{9,1},{2,10},{10,2},{3,11},{11,3},{4,12},{12,4},... | collective-permute-start | bytes 1179656 | tf_op jit(solution)/shard_map/ppermute | solution.py:273
  33.5 1.4 %stage.3.high_ref = bf16[256,3072]{1,0:T(8,128)(2,1)S(1)} custom-call(bf16[256,8192]{1,0:T(8,128)(2,1)} %tok_hbm.1), custom_call_target="tpu_custom_call" | custom-call | tf_op jit(solution)/shard_map/stage/pallas_call | solution.py:106
  34.9 0.0 collective-permute-done.1.theirs_ref
  34.9 1.9 %give.1 = (bf16[48,256]{1,0:T(8,128)(2,1)S(1)}, bf16[8,24,1024]{2,1,0:T(8,128)(2,1)S(1)}) custom-call(s32[1]{0:T(128)} %bitcast.core_ref, bf16[4,24,2048]{2,1,0:T(8,128)(2,1)S(1)} %all_to_all.15.mine_ref, bf16[4,24,2048]{2,1,0:T(8,128)(2,1)S(1)} %collective-permute-done.1.theirs_ref, bf16[48,256]{1,0:T(8,128)(2,1)S(1)} %bitcast.12, ...), custom_call_target="tpu_custom_call" | custom-call | tf_op jit(solution)/shard_map/give/pallas_call | solution.py:169
  36.8 2.2 %collective-permute-start.2 = (bf16[8,24,1024]{2,1,0:T(8,128)(2,1)S(1)}, bf16[8,24,1024]{2,1,0:T(8,128)(2,1)S(1)}, u32[]{:S(2)}, u32[]{:S(2)}) collective-permute-start(bf16[8,24,1024]{2,1,0:T(8,128)(2,1)S(1)} %get-tuple-element.20), channel_id=1, source_target_pairs={{0,8},{8,0},{1,9},{9,1},{2,10},{10,2},{3,11},{11,3},{4,12},{12,4},... | collective-permute-start | bytes 1179656 | tf_op jit(solution)/shard_map/ppermute | solution.py:278
  39.0 0.5 keep.1.kept_ref
  39.5 1.0 %collective-permute-done.2.got_ref = bf16[8,24,1024]{2,1,0:T(8,128)(2,1)S(1)} collective-permute-done((bf16[8,24,1024]{2,1,0:T(8,128)(2,1)S(1)}, bf16[8,24,1024]{2,1,0:T(8,128)(2,1)S(1)}, u32[]{:S(2)}, u32[]{:S(2)}) %collective-permute-start.2) | collective-permute-done | bytes 393248 | tf_op jit(solution)/shard_map/ppermute | solution.py:278
  40.4 0.1 add.1
  40.5 10.9 %all_to_all.16.in_ref = bf16[8,24,1024]{2,1,0:T(8,128)(2,1)S(1)} all-to-all(bf16[8,24,1024]{2,1,0:T(8,128)(2,1)S(1)} %add.1), channel_id=1, replica_groups=mesh['z_lo'=6,'y_hi'=4,'y_lo'=2,'core'=2,'z_hi'=2,'x'=4] {'y_lo','x'}, dimensions={0} | all-to-all | bytes 786432 | tf_op jit(solution)/shard_map/all_to_all | solution.py:281
  51.3 0.1 sum_peers.1
  51.4 25.8 %all_to_all.17 = bf16[48,4,128]{2,1,0:T(4,128)(2,1)S(1)} all-to-all(bf16[48,4,128]{2,1,0:T(4,128)(2,1)S(1)} %bitcast.10), channel_id=1, replica_groups=mesh['z_lo'=6,'y_hi'=4,'y_lo'=2,'core'=2,'z_hi'=2,'x'=4] {'z_lo','y_hi',..., dimensions={0} | all-to-all | bytes 98304 | tf_op jit(solution)/shard_map/all_to_all | solution.py:285
  77.3 0.6 final_sum.1
  (2 shorter events, 0.0 us)
Async XLA Ops:
  1.0 17.7 %collective-permute-start = (bf16[24,1024]{1,0:T(8,128)(2,1)S(1)}, bf16[24,1024]{1,0:T(8,128)(2,1)S(1)}, u32[]{:S(2)}, u32[]{:S(2)}) collective-permute-start(bf16[24,1024]{1,0:T(8,128)(2,1)S(1)} %prepare.1.mine_ref), channel_id=1, source_target_pairs={{0,388},{4,384},{128,516},{132,512},{256,644},{260,640},{384,4},{3... | collective-permute-start | bytes 147464 | tf_op jit(solution)/shard_map/ppermute | solution.py:265
  29.1 5.8 %collective-permute-start.1 = (bf16[4,24,2048]{2,1,0:T(8,128)(2,1)S(1)}, bf16[4,24,2048]{2,1,0:T(8,128)(2,1)S(1)}, u32[]{:S(2)}, u32[]{:S(2)}) collective-permute-start(bf16[4,24,2048]{2,1,0:T(8,128)(2,1)S(1)} %all_to_all.15.mine_ref), channel_id=1, source_target_pairs={{0,8},{8,0},{1,9},{9,1},{2,10},{10,2},{3,11},{11,3},{4,12},{12,4},... | collective-permute-start | bytes 1179656 | tf_op jit(solution)/shard_map/ppermute | solution.py:273
  36.8 3.6 %collective-permute-start.2 = (bf16[8,24,1024]{2,1,0:T(8,128)(2,1)S(1)}, bf16[8,24,1024]{2,1,0:T(8,128)(2,1)S(1)}, u32[]{:S(2)}, u32[]{:S(2)}) collective-permute-start(bf16[8,24,1024]{2,1,0:T(8,128)(2,1)S(1)} %get-tuple-element.20), channel_id=1, source_target_pairs={{0,8},{8,0},{1,9},{9,1},{2,10},{10,2},{3,11},{11,3},{4,12},{12,4},... | collective-permute-start | bytes 1179656 | tf_op jit(solution)/shard_map/ppermute | solution.py:278

commit v7 on v6

--- a/solution.py
+++ b/solution.py
@@ -34,11 +34,10 @@
     return sig * (1.0 + pre * (1.0 - sig))
 
 
-def prepare_kernel(core_ref, codes_hbm, scales_hbm, mine_ref, codes_ref, scales_ref, turned_ref, sems):
+def prepare_kernel(place_ref, codes_hbm, scales_hbm, mine_ref, codes_ref, scales_ref, turned_ref, sems):
+    core, y_lo = lax.rem(place_ref[0], CORE), lax.div(place_ref[0], CORE)
     copies = [
-        pltpu.make_async_copy(
-            codes_hbm.at[:, core_ref[0]], codes_ref, sems.at[0]
-        ),
+        pltpu.make_async_copy(codes_hbm.at[:, core], codes_ref, sems.at[0]),
         pltpu.make_async_copy(scales_hbm, scales_ref, sems.at[1]),
     ]
     for copy in copies:
@@ -49,18 +48,19 @@
     count = SHARD // BLOCK
     turned_ref[:, :count] = scales_ref[...].T
     even, odd = (turned_ref[pl.ds(y, HALF_ROWS, stride=Y_LO), :] for y in range(Y_LO))
-    scales = jnp.where(core_ref[0] == 0, even, odd)
-    for k in range(count):
-        block = slice(k * BLOCK, (k + 1) * BLOCK)
-        mine_ref[:, block] = (codes[:, block] * scales[:, k : k + 1]).astype(jnp.bfloat16)
-
-
-def prepare(core, w_codes, w_scales):
+    scales = jnp.where(core == 0, even, odd)
+    parts = [codes[:, k * BLOCK : (k + 1) * BLOCK] * scales[:, k : k + 1] for k in range(count)]
+    for k in range(count // Y_LO):
+        part = jnp.where(y_lo == 0, parts[k], parts[count // Y_LO + k])
+        mine_ref[:, k * BLOCK : (k + 1) * BLOCK] = part.astype(jnp.bfloat16)
+
+
+def prepare(place, w_codes, w_scales):
     w_codes = w_codes.reshape((HALF_ROWS, Y_LO) + w_codes.shape[1:])
     scales = w_scales.T
     return pl.pallas_call(
         prepare_kernel,
-        out_shape=jax.ShapeDtypeStruct((HALF_ROWS, SHARD), jnp.bfloat16),
+        out_shape=jax.ShapeDtypeStruct((HALF_ROWS, PIECE), jnp.bfloat16),
         in_specs=[SMEM, HBM, HBM],
         out_specs=VMEM,
         scratch_shapes=[
@@ -71,7 +71,7 @@
         ],
         compiler_params=pltpu.CompilerParams(vmem_limit_bytes=8 * 2**20),
         name="prepare",
-    )(core.reshape(1), in_hbm(w_codes), in_hbm(scales))
+    )(place.reshape(1), in_hbm(w_codes), in_hbm(scales))
 
 
 def spread_kernel(hi_ref, mine_ref, other_ref, out_ref):
@@ -79,15 +79,15 @@
     low = hi_ref[0] == 0
     first = jnp.where(low, mine, other)
     second = jnp.where(low, other, mine)
-    for x in range(X):
-        out_ref[x, :, :SHARD] = first
-        out_ref[x, :, SHARD:] = second
+    for peer in range(Y_LO * X):
+        out_ref[peer, :, :PIECE] = first
+        out_ref[peer, :, PIECE:] = second
 
 
 def spread(z_hi, mine, other):
     return pl.pallas_call(
         spread_kernel,
-        out_shape=jax.ShapeDtypeStruct((X, HALF_ROWS, Z_HI * SHARD), jnp.bfloat16),
+        out_shape=jax.ShapeDtypeStruct((Y_LO * X, HALF_ROWS, Z_HI * PIECE), jnp.bfloat16),
         in_specs=[SMEM, VMEM, VMEM],
         out_specs=VMEM,
         compiler_params=pltpu.CompilerParams(vmem_limit_bytes=8 * 2**20),
@@ -140,8 +140,12 @@
     pre = jnp.zeros((ROWS, cot_ref.shape[1]), jnp.float32)
     for hi in range(Z_HI):
         for x in range(X):
-            part = slice(hi * SHARD, (hi + 1) * SHARD)
-            rows = jnp.concatenate([mine_ref[x, :, part], theirs_ref[x, :, part]], axis=0)
+            part = slice(hi * PIECE, (hi + 1) * PIECE)
+            rows = [
+                jnp.concatenate([ref[y * X + x, :, part] for y in range(Y_LO)], axis=1)
+                for ref in (mine_ref, theirs_ref)
+            ]
+            rows = jnp.concatenate(rows, axis=0)
             pre += lax.dot_general(
                 rows,
                 columns_of(low_ref, high_ref, (hi * X + x) * SHARD, SHARD),
@@ -256,7 +260,7 @@
     core = lax.axis_index("core")
     z_hi = lax.axis_index("z_hi")
 
-    mine = prepare(core, w_codes, w_scales)
+    mine = prepare(core + CORE * lax.axis_index("y_lo"), w_codes, w_scales)
     shift = [
         (lo * Z_HI + hi, (lo + Z_LO // 2) % Z_LO * Z_HI + (1 - hi))
         for lo in range(Z_LO)
@@ -268,7 +272,7 @@
     cot = cotangent.T.reshape(HALF_ROWS, Y_LO, -1).transpose(1, 0, 2).reshape(ROWS, -1)
     copies = spread(z_hi, mine, other)
     copies, low, cot = lax.optimization_barrier((copies, low, cot))
-    half = lax.all_to_all(copies, "x", split_axis=0, concat_axis=0, tiled=True)
+    half = lax.all_to_all(copies, ("y_lo", "x"), split_axis=0, concat_axis=0, tiled=True)
 
     theirs = lax.ppermute(half, "core", SWAP)
     late_tokens, _ = lax.optimization_barrier((tokens, half))

time: 79.1 us -> 77.8 us (0.984)
  blocking collectives: 47.1 us -> 45.6 us
    all_to_all x1, blocking collectives: 25.8 us -> 23.5 us  [on_device(): lax.all_to_all(by_yz, ('z_lo', 'y_hi', 'z_hi'), split_axis=0, concat_axis...]
    all_to_all x1, blocking collectives: 10.4 us -> 11.8 us  [on_device(): lax.all_to_all(copies, ('y_lo', 'x'), split_axis=0, concat_axis=0, tiled=...]
where the time goes in v7:
time: 77.8 us; the launch traced here: 76.6 us
  blocking collectives  45.6 us (59%)
  starting transfers between devices  21.9 us (28%)
  Pallas kernels  7.32 us (9%)
  waiting for transfers between devices  0.96 us (1%)
    all_to_all x1, blocking collectives, on_device(): lax.all_to_all(by_yz, ('z_lo', 'y_hi', 'z_hi'), split_axis=0, concat_axis...  23.5 us
    ppermute x1, starting transfers between devices, on_device(): other = lax.ppermute(mine, ('z_lo', 'z_hi'), shift)  15.1 us
    all_to_all x1, blocking collectives, on_device(): lax.all_to_all(copies, ('y_lo', 'x'), split_axis=0, concat_axis=0, tiled=...  11.8 us
    all_to_all x1, blocking collectives, on_device(): lax.all_to_all(add(kept, got), ('y_lo', 'x'), split_axis=0, concat_axis=0...  10.4 us
    ppermute x1, starting transfers between devices, on_device(): theirs = lax.ppermute(half, 'core', SWAP)  4.58 us
    pallas_call x2, Pallas kernels, stage(): pl.pallas_call(functools.partial(stage_kernel, first=first), out_shape=pl...  3.17 us
    ppermute x1, starting transfers between devices, on_device(): got = lax.ppermute(given, 'core', SWAP)  2.18 us
    pallas_call x1, Pallas kernels, give(): pl.pallas_call(give_kernel, out_shape=[jax.ShapeDtypeStruct(cotangent.sha...  1.88 us
  transfers between devices with their start and end apart: 3, of which 1 were waited for; matrix products, arithmetic and copies ran while one was open for 1% of the time, Pallas kernels for 5%

profile of v7, /device:TPU:1, one launch (start us, length us, event | category | flops | bytes accessed | tf_op | source)
XLA Modules:
  0.0 76.6 jit_solution(7548181970096543806)
XLA Ops:
  0.0 1.0 %prepare.1.mine_ref = bf16[24,512]{1,0:T(8,128)(2,1)S(1)} custom-call(s32[1]{0:T(128)} %bitcast.2.place_ref, bf16[24,2,8,128]{3,2,1,0:T(8,128)(2,1)} %bitcast.14, f32[8,48]{1,0:T(8,128)} %bitcast.16), custom_call_target="tpu_custom_call" | custom-call | tf_op jit(solution)/shard_map/prepare/pallas_call | solution.py:61
  1.0 15.1 %collective-permute-start = (bf16[24,512]{1,0:T(8,128)(2,1)S(1)}, bf16[24,512]{1,0:T(8,128)(2,1)S(1)}, u32[]{:S(2)}, u32[]{:S(2)}) collective-permute-start(bf16[24,512]{1,0:T(8,128)(2,1)S(1)} %prepare.1.mine_ref), channel_id=1, source_target_pairs={{0,388},{4,384},{128,516},{132,512},{256,644},{260,640},{384,4},{3... | collective-permute-start | bytes 73736 | tf_op jit(solution)/shard_map/ppermute | solution.py:269
  16.2 0.8 reshape.29
  16.9 1.8 %stage.2.low_ref = bf16[256,5120]{1,0:T(8,128)(2,1)S(1)} custom-call(bf16[256,8192]{1,0:T(8,128)(2,1)} %tok_hbm.1), custom_call_target="tpu_custom_call" | custom-call | tf_op jit(solution)/shard_map/stage/pallas_call | solution.py:106
  18.7 0.0 collective-permute-done.other_ref
  18.7 11.8 %all_to_all.15.mine_ref = bf16[8,24,1024]{2,1,0:T(8,128)(2,1)S(1)} all-to-all(bf16[8,24,1024]{2,1,0:T(8,128)(2,1)S(1)} %spread.1), channel_id=1, replica_groups=mesh['z_lo'=6,'y_hi'=4,'y_lo'=2,'core'=2,'z_hi'=2,'x'=4] {'y_lo','x'}, dimensions={0} | all-to-all | bytes 786432 | tf_op jit(solution)/shard_map/all_to_all | solution.py:275
  30.5 4.6 %collective-permute-start.1 = (bf16[8,24,1024]{2,1,0:T(8,128)(2,1)S(1)}, bf16[8,24,1024]{2,1,0:T(8,128)(2,1)S(1)}, u32[]{:S(2)}, u32[]{:S(2)}) collective-permute-start(bf16[8,24,1024]{2,1,0:T(8,128)(2,1)S(1)} %all_to_all.15.mine_ref), channel_id=1, source_target_pairs={{0,8},{8,0},{1,9},{9,1},{2,10},{10,2},{3,11},{11,3},{4,12},{12,4},... | collective-permute-start | bytes 1179656 | tf_op jit(solution)/shard_map/ppermute | solution.py:277
  35.1 1.4 %stage.3.high_ref = bf16[256,3072]{1,0:T(8,128)(2,1)S(1)} custom-call(bf16[256,8192]{1,0:T(8,128)(2,1)} %tok_hbm.1), custom_call_target="tpu_custom_call" | custom-call | tf_op jit(solution)/shard_map/stage/pallas_call | solution.py:106
  36.5 0.0 collective-permute-done.1.theirs_ref
  36.5 1.9 %give.1 = (bf16[48,256]{1,0:T(8,128)(2,1)S(1)}, bf16[8,24,1024]{2,1,0:T(8,128)(2,1)S(1)}) custom-call(s32[1]{0:T(128)} %bitcast.core_ref, bf16[8,24,1024]{2,1,0:T(8,128)(2,1)S(1)} %all_to_all.15.mine_ref, bf16[8,24,1024]{2,1,0:T(8,128)(2,1)S(1)} %collective-permute-done.1.theirs_ref, bf16[48,256]{1,0:T(8,128)(2,1)S(1)} %bitcast.13, ...), custom_call_target="tpu_custom_call" | custom-call | tf_op jit(solution)/shard_map/give/pallas_call | solution.py:173
  38.4 2.2 %collective-permute-start.2 = (bf16[8,24,1024]{2,1,0:T(8,128)(2,1)S(1)}, bf16[8,24,1024]{2,1,0:T(8,128)(2,1)S(1)}, u32[]{:S(2)}, u32[]{:S(2)}) collective-permute-start(bf16[8,24,1024]{2,1,0:T(8,128)(2,1)S(1)} %get-tuple-element.20), channel_id=1, source_target_pairs={{0,8},{8,0},{1,9},{9,1},{2,10},{10,2},{3,11},{11,3},{4,12},{12,4},... | collective-permute-start | bytes 1179656 | tf_op jit(solution)/shard_map/ppermute | solution.py:282
  40.6 0.5 keep.1.kept_ref
  41.1 0.9 %collective-permute-done.2.got_ref = bf16[8,24,1024]{2,1,0:T(8,128)(2,1)S(1)} collective-permute-done((bf16[8,24,1024]{2,1,0:T(8,128)(2,1)S(1)}, bf16[8,24,1024]{2,1,0:T(8,128)(2,1)S(1)}, u32[]{:S(2)}, u32[]{:S(2)}) %collective-permute-start.2) | collective-permute-done | bytes 393248 | tf_op jit(solution)/shard_map/ppermute | solution.py:282
  42.0 0.1 add.5
  42.1 10.4 %all_to_all.16.in_ref = bf16[8,24,1024]{2,1,0:T(8,128)(2,1)S(1)} all-to-all(bf16[8,24,1024]{2,1,0:T(8,128)(2,1)S(1)} %add.5), channel_id=1, replica_groups=mesh['z_lo'=6,'y_hi'=4,'y_lo'=2,'core'=2,'z_hi'=2,'x'=4] {'y_lo','x'}, dimensions={0} | all-to-all | bytes 786432 | tf_op jit(solution)/shard_map/all_to_all | solution.py:285
  52.5 0.1 sum_peers.1
  52.5 23.5 %all_to_all.17 = bf16[48,4,128]{2,1,0:T(4,128)(2,1)S(1)} all-to-all(bf16[48,4,128]{2,1,0:T(4,128)(2,1)S(1)} %bitcast.11), channel_id=1, replica_groups=mesh['z_lo'=6,'y_hi'=4,'y_lo'=2,'core'=2,'z_hi'=2,'x'=4] {'z_lo','y_hi',..., dimensions={0} | all-to-all | bytes 98304 | tf_op jit(solution)/shard_map/all_to_all | solution.py:289
  76.0 0.6 final_sum.1
  (2 shorter events, 0.0 us)
Async XLA Ops:
  1.0 17.7 %collective-permute-start = (bf16[24,512]{1,0:T(8,128)(2,1)S(1)}, bf16[24,512]{1,0:T(8,128)(2,1)S(1)}, u32[]{:S(2)}, u32[]{:S(2)}) collective-permute-start(bf16[24,512]{1,0:T(8,128)(2,1)S(1)} %prepare.1.mine_ref), channel_id=1, source_target_pairs={{0,388},{4,384},{128,516},{132,512},{256,644},{260,640},{384,4},{3... | collective-permute-start | bytes 73736 | tf_op jit(solution)/shard_map/ppermute | solution.py:269
  30.5 6.0 %collective-permute-start.1 = (bf16[8,24,1024]{2,1,0:T(8,128)(2,1)S(1)}, bf16[8,24,1024]{2,1,0:T(8,128)(2,1)S(1)}, u32[]{:S(2)}, u32[]{:S(2)}) collective-permute-start(bf16[8,24,1024]{2,1,0:T(8,128)(2,1)S(1)} %all_to_all.15.mine_ref), channel_id=1, source_target_pairs={{0,8},{8,0},{1,9},{9,1},{2,10},{10,2},{3,11},{11,3},{4,12},{12,4},... | collective-permute-start | bytes 1179656 | tf_op jit(solution)/shard_map/ppermute | solution.py:277
  38.4 3.6 %collective-permute-start.2 = (bf16[8,24,1024]{2,1,0:T(8,128)(2,1)S(1)}, bf16[8,24,1024]{2,1,0:T(8,128)(2,1)S(1)}, u32[]{:S(2)}, u32[]{:S(2)}) collective-permute-start(bf16[8,24,1024]{2,1,0:T(8,128)(2,1)S(1)} %get-tuple-element.20), channel_id=1, source_target_pairs={{0,8},{8,0},{1,9},{9,1},{2,10},{10,2},{3,11},{11,3},{4,12},{12,4},... | collective-permute-start | bytes 1179656 | tf_op jit(solution)/shard_map/ppermute | solution.py:282
